TPU v7x, 128 devices: a whole 4x4x4 slice. The times are simulated.
128 devices in a mesh: ctx: 32 (over y, z_hi, x), dp: 4 (over z_lo, core).
Axes of the slice: x: 4, y: 4, z: 4 (z_hi: 2, z_lo: 2; z = z_hi * 2 + z_lo), core: 2. Of those that a mesh axis runs over, the one named last changes fastest.
Arguments:
- queries: bfloat16 [4, 4096, 12288], P('dp', 'ctx'), may hold values from -6 to 6
- latents: bfloat16 [4, 4096, 576], P('dp', 'ctx'), may hold values from -6 to 6
- cotangent: bfloat16 [4, 4096, 8192], P('dp', 'ctx'), may hold values from -6 to 6
- offsets: float32 [4, 64, 4096], P('dp', None, 'ctx'), may hold values from 2 to 4
- corrections: float32 [4, 64, 4096], P('dp', None, 'ctx'), may hold values from -24 to 24
- span_order: int32 [4, 64], P('dp'), may hold values from 0 to 63, each once within a row
- latent_gain: float32 [512], replicated, may hold values from 0.1 to 1.9
- up_weight: bfloat16 [512, 16384], replicated, may hold values from -0.25 to 0.25
Outputs:
- grad_query: bfloat16 [4, 4096, 12288], P('dp', 'ctx')
- grad_latent: float32 [4, 4096, 576], P('dp', 'ctx')
- grad_gain: float32 [512], replicated
Inputs may be any that keep to these rules, and one draw needn't show every extreme that they name: Each row of span_order names every block of the sequence exactly once.
All inputs are finite; a program needn't handle non-finite values.
Results may differ from a plain program's by a relative error of at most 0.012.
The roundings to bfloat16 on the way count: a program that leaves them out, or rounds other values in their place, can miss the bound.
Values may be sent and summed in bfloat16 or wider, within the bound.
No kernel may reach another device: no remote copies, remote signals or barrier semaphores. Data moves between devices by JAX's collectives and lax.ppermute only.
A program may use at most 256 MiB of HBM per device.

v0:
```python
import functools
import jax
import jax.numpy as jnp
from jax import lax
from jax.experimental import pallas as pl
from jax.experimental.pallas import tpu as pltpu
from jax.sharding import PartitionSpec as P

H = 64
KVL = 512
DR = 64
DN = 128
DV = 128
STEPS = 5
HB = 2
TOK = 128
N_CTX = 32
SCALE = (DN + DR) ** -0.5
LOG2E = 1.4426950408889634
F32 = jnp.float32
BF16 = jnp.bfloat16


def dot_t(a, b):
    return lax.dot_general(a, b, (((1,), (1,)), ((), ())), preferred_element_type=F32)


def dot_l(a, b):
    return lax.dot_general(a, b, (((0,), (0,)), ((), ())), preferred_element_type=F32)


def dot_n(a, b):
    return jnp.dot(a, b, preferred_element_type=F32)


def kernel(steps, order, member, gain, offs, corr, *refs):
    n = len(steps)
    lats = refs[:n]
    w, q, cot, dq = refs[n : n + 4]
    grads = refs[n + 4 : 2 * n + 4]
    gain_part = refs[2 * n + 4]
    scaled, rope, bias, acc, racc, mul = refs[2 * n + 5 :]
    step = pl.program_id(0)
    half = TOK // 2

    @pl.when(step == 0)
    def _():
        rows = lax.broadcasted_iota(jnp.int32, (TOK, TOK), 0)
        cols = lax.broadcasted_iota(jnp.int32, (TOK, TOK), 1)
        own = member[0]

        def positions(index, group):
            block = jnp.where(index < half, order[0, 2 * group], order[0, 2 * group + 1])
            return block * half + lax.rem(index, half)

        qpos = positions(cols, own)
        for i, s in enumerate(steps):
            group = lax.rem(own + N_CTX - s, N_CTX)
            kpos = positions(rows, group)
            part = pl.ds(i * TOK, TOK)
            bias[part, :] = jnp.where(kpos <= qpos, 0.0, -1e30)
            tile = lats[i][...].astype(F32).T
            scaled[part, :] = (tile[:, :KVL] * gain[...]).astype(BF16)
            rope[part, :] = tile[:, KVL:].astype(BF16)
        acc[...] = jnp.zeros_like(acc)
        racc[...] = jnp.zeros_like(racc)

    rot = jnp.concatenate([q[:, DN : DN + DR], q[:, 2 * DN + DR :]], 0)
    proj = dot_n(scaled[...], w[...]).astype(BF16)
    srot = dot_t(rope[...], rot)
    zero = jnp.zeros((TOK, TOK), BF16)
    dss, dkvs = [], []
    for i in range(HB):
        qn = q[:, i * (DN + DR) : i * (DN + DR) + DN]
        ct = cot[:, i * DV : (i + 1) * DV]
        diag = jnp.concatenate(
            [jnp.concatenate([qn, zero], 1), jnp.concatenate([zero, ct], 1)], 0
        )
        head = step * HB + i
        off = offs[pl.ds(head, 1), :] * LOG2E
        cor = corr[pl.ds(head, 1), :]
        ph = proj[:, i * 256 : (i + 1) * 256]
        sd = dot_t(ph, diag)
        s = sd[:, :TOK] + srot[:, i * TOK : (i + 1) * TOK]
        p = jnp.exp2(s * (SCALE * LOG2E) + (bias[...] - off))
        ds = (p * (sd[:, TOK:] - cor)).astype(BF16)
        pb = p.astype(BF16)
        dkv = dot_n(jnp.concatenate([ds, pb], 1), diag)
        dkvs.append((dkv * mul[...]).astype(BF16))
        dss.append(ds)
        kr = jnp.concatenate([ph[:, :DN], rope[...]], 1)
        dq[:, i * (DN + DR) : (i + 1) * (DN + DR)] = (dot_l(ds, kr) * SCALE).astype(BF16)
    racc[...] += dot_n(jnp.concatenate(dss, 1), rot)
    acc[...] += dot_t(jnp.concatenate(dkvs, 1), w[...])

    @pl.when(step == H // HB - 1)
    def _():
        total = jnp.zeros((1, KVL), F32)
        for i in range(n):
            part = pl.ds(i * TOK, TOK)
            g = acc[part, :]
            tile = lats[i][:KVL, :].astype(F32).T
            total = total + jnp.sum(g * tile, axis=0, keepdims=True)
            grads[i][:KVL, :] = g.T
            grads[i][KVL:, :] = (racc[part, :] * SCALE).T
        gain_part[...] = total


def visits(steps, order, member, gain, offs, corr, lats, w, q, cot):
    n = len(steps)
    rows = n * TOK
    vm = pl.BlockSpec(memory_space=pltpu.VMEM)
    sm = pl.BlockSpec(memory_space=pltpu.SMEM)
    mul = jnp.concatenate([jnp.full((1, DN), SCALE, F32), jnp.ones((1, DV), F32)], 1)
    full = lambda *s: pl.BlockSpec(s, lambda i: (0,) * len(s))
    return pl.pallas_call(
        functools.partial(kernel_mul, steps),
        grid=(H // HB,),
        out_shape=[jax.ShapeDtypeStruct((TOK, H * (DN + DR)), BF16)]
        + [jax.ShapeDtypeStruct((KVL + DR, TOK), F32)] * n
        + [jax.ShapeDtypeStruct((1, KVL), F32)],
        in_specs=[sm, sm, full(1, KVL), full(H, TOK), full(H, TOK)]
        + [full(KVL + DR, TOK)] * n
        + [
            pl.BlockSpec((KVL, HB * (DN + DV)), lambda i: (0, i)),
            pl.BlockSpec((TOK, HB * (DN + DR)), lambda i: (0, i)),
            pl.BlockSpec((TOK, HB * DV), lambda i: (0, i)),
            full(1, DN + DV),
        ],
        out_specs=[pl.BlockSpec((TOK, HB * (DN + DR)), lambda i: (0, i))]
        + [full(KVL + DR, TOK)] * n
        + [full(1, KVL)],
        scratch_shapes=[
            pltpu.VMEM((rows, KVL), BF16),
            pltpu.VMEM((rows, DR), BF16),
            pltpu.VMEM((rows, TOK), F32),
            pltpu.VMEM((rows, KVL), F32),
            pltpu.VMEM((rows, DR), F32),
        ],
        compiler_params=pltpu.CompilerParams(vmem_limit_bytes=60 * 2**20, dimension_semantics=("arbitrary",)),
    )(order, member, gain, offs, corr, *lats, w, q, cot, mul)


def kernel_mul(steps, *refs):
    n = len(steps)
    mul = refs[5 + n + 3]
    rest = refs[: 5 + n + 3] + refs[5 + n + 4 :]
    kernel(steps, *rest, mul)


def xor_sum(x, bits):
    parts = [x]
    for bit in bits:
        parts = parts + [
            lax.ppermute(x, "ctx", [(i, i ^ (bit ^ done)) for i in range(lax.axis_size("ctx"))])
            for done in shifts(bits, bit)
        ]
    while len(parts) > 1:
        parts = [a + b for a, b in zip(parts[::2], parts[1::2])]
    return parts[0]


def shifts(bits, bit):
    low = [0]
    for other in bits:
        if other == bit:
            break
        low = low + [v ^ other for v in low]
    return low


def moved(x, distance):
    n = lax.axis_size("ctx")
    return lax.ppermute(x, "ctx", [((i - distance) % n, i) for i in range(n)])


def body(queries, latents, cotangent, offsets, corrections, span_order, latent_gain, up_weight):
    own = latents[0].T
    member = lax.axis_index("ctx").astype(jnp.int32).reshape(1)
    lats = [own] + [moved(own, s) for s in range(1, STEPS)]
    dq, *grads, gain_part = visits(
        tuple(range(STEPS)),
        span_order,
        member,
        latent_gain[None],
        offsets[0],
        corrections[0],
        lats,
        up_weight,
        queries[0],
        cotangent[0],
    )
    back = [moved(grads[s], -s) for s in range(1, STEPS)]
    gain_sum = lax.psum(gain_part[0], "dp")
    for bits in ((1, 2), (4,), (8, 16)):
        gain_sum = xor_sum(gain_sum, bits)
    total = grads[0] + ((back[0] + back[1]) + (back[2] + back[3]))
    factor = jnp.concatenate([latent_gain, jnp.ones((DR,), F32)])
    return dq[None], (total * factor[:, None]).T[None], gain_sum


def solution(mesh):
    in_specs = (
        P("dp", "ctx", None),
        P("dp", "ctx", None),
        P("dp", "ctx", None),
        P("dp", None, "ctx"),
        P("dp", None, "ctx"),
        P("dp", None),
        P(),
        P(),
    )
    out_specs = (P("dp", "ctx", None), P("dp", "ctx", None), P())
    return jax.shard_map(body, mesh=mesh, in_specs=in_specs, out_specs=out_specs, check_vma=False)
```

profile of v0, /device:TPU:6, one launch (start us, length us, event | category | flops | bytes accessed | tf_op | source)
XLA Modules:
  0.0 141.4 jit_solution(7323868660070682852)
XLA Ops:
  0.6 3.9 %collective-permute-start = (bf16[576,128]{1,0:T(8,128)(2,1)}, bf16[576,128]{1,0:T(8,128)(2,1)S(1)}, u32[]{:S(2)}, u32[]{:S(2)}) collective-permute-start(bf16[576,128]{1,0:T(8,128)(2,1)} %bitcast.17), channel_id=1, source_target_pairs={{124,0},{0,4},{4,8},{8,12},{12,16},{16,20},{20,24},{24,28},{28,32}... | collective-permute-start | bytes 442376 | tf_op jit(solution)/shard_map/ppermute | solution.py:174
  4.5 2.4 %collective-permute-start.1 = (bf16[576,128]{1,0:T(8,128)(2,1)}, bf16[576,128]{1,0:T(8,128)(2,1)S(1)}, u32[]{:S(2)}, u32[]{:S(2)}) collective-permute-start(bf16[576,128]{1,0:T(8,128)(2,1)} %bitcast.18), channel_id=1, source_target_pairs={{120,0},{124,4},{0,8},{4,12},{8,16},{12,20},{16,24},{20,28},{24,32... | collective-permute-start | bytes 442376 | tf_op jit(solution)/shard_map/ppermute | solution.py:174
  6.9 0.0 collective-permute-start.2
  6.9 3.9 %collective-permute-start.3 = (bf16[576,128]{1,0:T(8,128)(2,1)}, bf16[576,128]{1,0:T(8,128)(2,1)S(1)}, u32[]{:S(2)}, u32[]{:S(2)}) collective-permute-start(bf16[576,128]{1,0:T(8,128)(2,1)} %bitcast.20), channel_id=1, source_target_pairs={{112,0},{116,4},{120,8},{124,12},{0,16},{4,20},{8,24},{12,28},{16,... | collective-permute-start | bytes 442376 | tf_op jit(solution)/shard_map/ppermute | solution.py:174
  10.8 1.1 collective-permute-done.refs_6_
  12.0 0.0 copy-start
  12.0 0.8 collective-permute-done.1.refs_7_
  12.8 0.0 copy-start.1
  12.8 1.9 %collective-permute-done.2.refs_8_ = bf16[576,128]{1,0:T(8,128)(2,1)S(1)} collective-permute-done((bf16[576,128]{1,0:T(8,128)(2,1)}, bf16[576,128]{1,0:T(8,128)(2,1)S(1)}, u32[]{:S(2)}, u32[]{:S(2)}) %collective-permute-start.2) | collective-permute-done | bytes 147488 | tf_op jit(solution)/shard_map/ppermute | solution.py:174
  14.7 0.0 copy-start.2
  14.7 1.2 collective-permute-done.3.refs_9_
  15.9 0.0 copy-start.3
  15.9 0.0 copy-done
  15.9 0.0 copy-done.1
  15.9 0.0 copy-done.2
  15.9 0.7 copy-done.3
  16.6 0.0 copy-start.4
  16.6 63.1 %shard_map.103 = (bf16[128,12288]{1,0:T(8,128)(2,1)}, f32[576,128]{1,0:T(8,128)}, f32[576,128]{1,0:T(8,128)}, f32[576,128]{1,0:T(8,128)}, f32[576,128]{1,0:T(8,1...) custom-call(s32[1,64]{1,0:T(1,128)} %refs_0_.1, s32[1]{0:T(128)} %bitcast.refs_1_, f32[1,512]{1,0:T(1,128)} %bitcast.24, ...), custom_call_target="tpu_custom_call" | custom-call | tf_op jit(solution)/shard_map/pallas_call | solution.py:116
  79.7 5.8 %psum.7 = f32[512]{0:T(512)S(1)} all-reduce(f32[512]{0:T(512)} %bitcast.25), channel_id=1, replica_groups=mesh['ctx'=32,'dp'=4] {'dp'}, use_global_device_ids=true, to_apply=%region_0.0 | all-reduce | flops 512 | bytes 4096 | tf_op jit(solution)/shard_map/psum | solution.py:194
  85.5 8.1 %collective-permute-start.10 = (f32[512]{0:T(512)S(1)}, f32[512]{0:T(512)S(1)}, u32[]{:S(2)}, u32[]{:S(2)}) collective-permute-start(f32[512]{0:T(512)S(1)} %psum.7), channel_id=1, source_target_pairs={{0,12},{4,8},{8,4},{12,0},{16,28},{20,24},{24,20},{28,16},{32,44},... | collective-permute-start | bytes 6152 | tf_op jit(solution)/shard_map/ppermute | solution.py:155
  93.6 0.0 collective-permute-start.8
  93.6 1.6 %collective-permute-start.9 = (f32[512]{0:T(512)S(1)}, f32[512]{0:T(512)S(1)}, u32[]{:S(2)}, u32[]{:S(2)}) collective-permute-start(f32[512]{0:T(512)S(1)} %psum.7), channel_id=1, source_target_pairs={{0,8},{4,12},{8,0},{12,4},{16,24},{20,28},{24,16},{28,20},{32,40},... | collective-permute-start | bytes 6152 | tf_op jit(solution)/shard_map/ppermute | solution.py:155
  95.2 0.5 collective-permute-start.4
  95.7 4.1 %collective-permute-start.5 = (f32[576,128]{1,0:T(8,128)}, f32[576,128]{1,0:T(8,128)S(1)}, u32[]{:S(2)}, u32[]{:S(2)}) collective-permute-start(f32[576,128]{1,0:T(8,128)} %get-tuple-element.13), channel_id=1, source_target_pairs={{8,0},{12,4},{16,8},{20,12},{24,16},{28,20},{32,24},{36,28},{40,32... | collective-permute-start | bytes 884744 | tf_op jit(solution)/shard_map/ppermute | solution.py:174
  99.8 0.0 collective-permute-done.10
  99.8 3.2 %collective-permute-start.6 = (f32[576,128]{1,0:T(8,128)}, f32[576,128]{1,0:T(8,128)S(1)}, u32[]{:S(2)}, u32[]{:S(2)}) collective-permute-start(f32[576,128]{1,0:T(8,128)} %get-tuple-element.14), channel_id=1, source_target_pairs={{12,0},{16,4},{20,8},{24,12},{28,16},{32,20},{36,24},{40,28},{44,3... | collective-permute-start | bytes 884744 | tf_op jit(solution)/shard_map/ppermute | solution.py:174
  103.0 0.0 collective-permute-done.8
  103.0 0.8 collective-permute-start.7
  103.8 0.0 collective-permute-done.9
  103.9 2.8 %collective-permute-start.11 = (f32[512]{0:T(512)S(1)}, f32[512]{0:T(512)S(1)}, u32[]{:S(2)}, u32[]{:S(2)}) collective-permute-start(f32[512]{0:T(512)S(1)} %add_add_fusion.1), channel_id=1, source_target_pairs={{0,16},{4,20},{8,24},{12,28},{16,0},{20,4},{24,8},{28,12},{32,48},... | collective-permute-start | bytes 6152 | tf_op jit(solution)/shard_map/ppermute | solution.py:155
  106.6 18.9 %collective-permute-done.11 = f32[512]{0:T(512)S(1)} collective-permute-done((f32[512]{0:T(512)S(1)}, f32[512]{0:T(512)S(1)}, u32[]{:S(2)}, u32[]{:S(2)}) %collective-permute-start.11) | collective-permute-done | bytes 2080 | tf_op jit(solution)/shard_map/ppermute | solution.py:155
  125.5 0.0 collective-permute-start.12
  125.5 3.6 %collective-permute-done.12 = f32[512]{0:T(512)S(1)} collective-permute-done((f32[512]{0:T(512)S(1)}, f32[512]{0:T(512)S(1)}, u32[]{:S(2)}, u32[]{:S(2)}) %collective-permute-start.12) | collective-permute-done | bytes 2080 | tf_op jit(solution)/shard_map/ppermute | solution.py:155
  129.1 1.2 collective-permute-start.13
  130.3 3.8 %collective-permute-done.13 = f32[512]{0:T(512)S(1)} collective-permute-done((f32[512]{0:T(512)S(1)}, f32[512]{0:T(512)S(1)}, u32[]{:S(2)}, u32[]{:S(2)}) %collective-permute-start.13) | collective-permute-done | bytes 2080 | tf_op jit(solution)/shard_map/ppermute | solution.py:155
  134.2 1.1 collective-permute-start.14
  135.2 0.0 copy-done.4
  135.2 3.7 %collective-permute-done.14 = f32[512]{0:T(512)S(1)} collective-permute-done((f32[512]{0:T(512)S(1)}, f32[512]{0:T(512)S(1)}, u32[]{:S(2)}, u32[]{:S(2)}) %collective-permute-start.14) | collective-permute-done | bytes 2080 | tf_op jit(solution)/shard_map/ppermute | solution.py:155
  139.0 0.6 add_add_fusion
  139.6 0.0 collective-permute-done.4
  139.6 0.0 collective-permute-done.5
  139.6 0.0 collective-permute-done.6
  139.6 0.0 collective-permute-done.7
  139.6 1.8 %multiply_bitcast_fusion = f32[1,128,576]{1,2,0:T(8,128)} fusion(f32[576,128]{1,0:T(8,128)} %get-tuple-element.11, f32[576,128]{1,0:T(8,128)S(1)} %collective-permute-done.6, f32[576,128]{1,0:T(8,128)S(1)} %collective-permute-done.7, f32[576,128]{1,0:T(8,128)S(1)} %collective-permute-done.4, f32[576,128]{1,0:T(8,128)S(1)} %collective-permute-done.5, ...), kind=kLoop, calls=%fused_computation | loop fusion | flops 368640 | bytes 1771776 | tf_op jit(solution)/shard_map/broadcast_in_dim | solution.py:199
  (3 shorter events, 0.0 us)
Async XLA Ops:
  0.6 11.3 %collective-permute-start = (bf16[576,128]{1,0:T(8,128)(2,1)}, bf16[576,128]{1,0:T(8,128)(2,1)S(1)}, u32[]{:S(2)}, u32[]{:S(2)}) collective-permute-start(bf16[576,128]{1,0:T(8,128)(2,1)} %bitcast.17), channel_id=1, source_target_pairs={{124,0},{0,4},{4,8},{8,12},{12,16},{16,20},{20,24},{24,28},{28,32}... | collective-permute-start | bytes 442376 | tf_op jit(solution)/shard_map/ppermute | solution.py:174
  4.5 8.3 %collective-permute-start.1 = (bf16[576,128]{1,0:T(8,128)(2,1)}, bf16[576,128]{1,0:T(8,128)(2,1)S(1)}, u32[]{:S(2)}, u32[]{:S(2)}) collective-permute-start(bf16[576,128]{1,0:T(8,128)(2,1)} %bitcast.18), channel_id=1, source_target_pairs={{120,0},{124,4},{0,8},{4,12},{8,16},{12,20},{16,24},{20,28},{24,32... | collective-permute-start | bytes 442376 | tf_op jit(solution)/shard_map/ppermute | solution.py:174
  6.9 7.8 %collective-permute-start.2 = (bf16[576,128]{1,0:T(8,128)(2,1)}, bf16[576,128]{1,0:T(8,128)(2,1)S(1)}, u32[]{:S(2)}, u32[]{:S(2)}) collective-permute-start(bf16[576,128]{1,0:T(8,128)(2,1)} %bitcast.19), channel_id=1, source_target_pairs={{116,0},{120,4},{124,8},{0,12},{4,16},{8,20},{12,24},{16,28},{20,3... | collective-permute-start | bytes 442376 | tf_op jit(solution)/shard_map/ppermute | solution.py:174
  6.9 9.0 %collective-permute-start.3 = (bf16[576,128]{1,0:T(8,128)(2,1)}, bf16[576,128]{1,0:T(8,128)(2,1)S(1)}, u32[]{:S(2)}, u32[]{:S(2)}) collective-permute-start(bf16[576,128]{1,0:T(8,128)(2,1)} %bitcast.20), channel_id=1, source_target_pairs={{112,0},{116,4},{120,8},{124,12},{0,16},{4,20},{8,24},{12,28},{16,... | collective-permute-start | bytes 442376 | tf_op jit(solution)/shard_map/ppermute | solution.py:174
  12.0 4.0 %copy-start = (bf16[576,128]{1,0:T(8,128)(2,1)}, bf16[576,128]{1,0:T(8,128)(2,1)S(1)}, u32[]{:S(2)}) copy-start(bf16[576,128]{1,0:T(8,128)(2,1)S(1)} %collective-permute-done.refs_6_) | copy-start | bytes 442372
  12.8 3.1 %copy-start.1 = (bf16[576,128]{1,0:T(8,128)(2,1)}, bf16[576,128]{1,0:T(8,128)(2,1)S(1)}, u32[]{:S(2)}) copy-start(bf16[576,128]{1,0:T(8,128)(2,1)S(1)} %collective-permute-done.1.refs_7_) | copy-start | bytes 442372
  14.7 1.2 copy-start.2
  15.9 0.7 copy-start.3
  16.6 118.7 %copy-start.4 = (f32[512]{0:T(512)S(1)}, f32[512]{0:T(512)}, u32[]{:S(2)}) copy-start(f32[512]{0:T(512)} %param.14) | copy-start | bytes 6148
  85.5 14.3 %collective-permute-start.10 = (f32[512]{0:T(512)S(1)}, f32[512]{0:T(512)S(1)}, u32[]{:S(2)}, u32[]{:S(2)}) collective-permute-start(f32[512]{0:T(512)S(1)} %psum.7), channel_id=1, source_target_pairs={{0,12},{4,8},{8,4},{12,0},{16,28},{20,24},{24,20},{28,16},{32,44},... | collective-permute-start | bytes 6152 | tf_op jit(solution)/shard_map/ppermute | solution.py:155
  93.6 9.4 %collective-permute-start.8 = (f32[512]{0:T(512)S(1)}, f32[512]{0:T(512)S(1)}, u32[]{:S(2)}, u32[]{:S(2)}) collective-permute-start(f32[512]{0:T(512)S(1)} %psum.7), channel_id=1, source_target_pairs={{0,4},{4,0},{8,12},{12,8},{16,20},{20,16},{24,28},{28,24},{32,36},... | collective-permute-start | bytes 6152 | tf_op jit(solution)/shard_map/ppermute | solution.py:155
  93.6 10.2 %collective-permute-start.9 = (f32[512]{0:T(512)S(1)}, f32[512]{0:T(512)S(1)}, u32[]{:S(2)}, u32[]{:S(2)}) collective-permute-start(f32[512]{0:T(512)S(1)} %psum.7), channel_id=1, source_target_pairs={{0,8},{4,12},{8,0},{12,4},{16,24},{20,28},{24,16},{28,20},{32,40},... | collective-permute-start | bytes 6152 | tf_op jit(solution)/shard_map/ppermute | solution.py:155
  95.2 44.4 %collective-permute-start.4 = (f32[576,128]{1,0:T(8,128)}, f32[576,128]{1,0:T(8,128)S(1)}, u32[]{:S(2)}, u32[]{:S(2)}) collective-permute-start(f32[576,128]{1,0:T(8,128)} %get-tuple-element.12), channel_id=1, source_target_pairs={{4,0},{8,4},{12,8},{16,12},{20,16},{24,20},{28,24},{32,28},{36,32}... | collective-permute-start | bytes 884744 | tf_op jit(solution)/shard_map/ppermute | solution.py:174
  95.7 43.9 %collective-permute-start.5 = (f32[576,128]{1,0:T(8,128)}, f32[576,128]{1,0:T(8,128)S(1)}, u32[]{:S(2)}, u32[]{:S(2)}) collective-permute-start(f32[576,128]{1,0:T(8,128)} %get-tuple-element.13), channel_id=1, source_target_pairs={{8,0},{12,4},{16,8},{20,12},{24,16},{28,20},{32,24},{36,28},{40,32... | collective-permute-start | bytes 884744 | tf_op jit(solution)/shard_map/ppermute | solution.py:174
  99.8 39.8 %collective-permute-start.6 = (f32[576,128]{1,0:T(8,128)}, f32[576,128]{1,0:T(8,128)S(1)}, u32[]{:S(2)}, u32[]{:S(2)}) collective-permute-start(f32[576,128]{1,0:T(8,128)} %get-tuple-element.14), channel_id=1, source_target_pairs={{12,0},{16,4},{20,8},{24,12},{28,16},{32,20},{36,24},{40,28},{44,3... | collective-permute-start | bytes 884744 | tf_op jit(solution)/shard_map/ppermute | solution.py:174
  103.0 36.6 %collective-permute-start.7 = (f32[576,128]{1,0:T(8,128)}, f32[576,128]{1,0:T(8,128)S(1)}, u32[]{:S(2)}, u32[]{:S(2)}) collective-permute-start(f32[576,128]{1,0:T(8,128)} %get-tuple-element.15), channel_id=1, source_target_pairs={{16,0},{20,4},{24,8},{28,12},{32,16},{36,20},{40,24},{44,28},{48,3... | collective-permute-start | bytes 884744 | tf_op jit(solution)/shard_map/ppermute | solution.py:174
  103.9 21.6 %collective-permute-start.11 = (f32[512]{0:T(512)S(1)}, f32[512]{0:T(512)S(1)}, u32[]{:S(2)}, u32[]{:S(2)}) collective-permute-start(f32[512]{0:T(512)S(1)} %add_add_fusion.1), channel_id=1, source_target_pairs={{0,16},{4,20},{8,24},{12,28},{16,0},{20,4},{24,8},{28,12},{32,48},... | collective-permute-start | bytes 6152 | tf_op jit(solution)/shard_map/ppermute | solution.py:155
  125.5 3.6 %collective-permute-start.12 = (f32[512]{0:T(512)S(1)}, f32[512]{0:T(512)S(1)}, u32[]{:S(2)}, u32[]{:S(2)}) collective-permute-start(f32[512]{0:T(512)S(1)} %add.44), channel_id=1, source_target_pairs={{0,32},{4,36},{8,40},{12,44},{16,48},{20,52},{24,56},{28,60},{32,0... | collective-permute-start | bytes 6152 | tf_op jit(solution)/shard_map/ppermute | solution.py:155
  129.1 5.1 %collective-permute-start.13 = (f32[512]{0:T(512)S(1)}, f32[512]{0:T(512)S(1)}, u32[]{:S(2)}, u32[]{:S(2)}) collective-permute-start(f32[512]{0:T(512)S(1)} %add.44), channel_id=1, source_target_pairs={{0,64},{4,68},{8,72},{12,76},{16,80},{20,84},{24,88},{28,92},{32,9... | collective-permute-start | bytes 6152 | tf_op jit(solution)/shard_map/ppermute | solution.py:155
  134.2 4.8 %collective-permute-start.14 = (f32[512]{0:T(512)S(1)}, f32[512]{0:T(512)S(1)}, u32[]{:S(2)}, u32[]{:S(2)}) collective-permute-start(f32[512]{0:T(512)S(1)} %add.44), channel_id=1, source_target_pairs={{0,96},{4,100},{8,104},{12,108},{16,112},{20,116},{24,120},{28,124... | collective-permute-start | bytes 6152 | tf_op jit(solution)/shard_map/ppermute | solution.py:155
where the time goes:
time: 142 us; the launch traced here: 141 us
  Pallas kernels  63.1 us (44%)
  waiting for transfers between devices  35.1 us (25%)
  starting transfers between devices  33.6 us (24%)
  blocking collectives  5.8 us (4%)
  other arithmetic  2.41 us (2%)
    pallas_call x1, Pallas kernels, visits(): pl.pallas_call(functools.partial(kernel_mul, steps), grid=(H // HB,), out...  63.1 us
    ppermute x7, waiting for transfers between devices, xor_sum(): lax.ppermute(x, 'ctx', [(i, i ^ (bit ^ done)) for i in range(lax.axis_siz...  30 us
    ppermute x8, starting transfers between devices, moved(): return lax.ppermute(x, 'ctx', [((i - distance) % n, i) for i in range(n)])  18.8 us
    ppermute x7, starting transfers between devices, xor_sum(): lax.ppermute(x, 'ctx', [(i, i ^ (bit ^ done)) for i in range(lax.axis_siz...  14.7 us
    psum x1, blocking collectives, body(): gain_sum = lax.psum(gain_part[0], 'dp')  5.8 us
    ppermute x8, waiting for transfers between devices, moved(): return lax.ppermute(x, 'ctx', [((i - distance) % n, i) for i in range(n)])  5.09 us
  transfers between devices with their start and end apart: 15, of which 8 were waited for; matrix products, arithmetic and copies ran while one was open for 0% of the time, Pallas kernels for 0%

commit v1 on v0

--- a/solution.py
+++ b/solution.py
@@ -12,7 +12,7 @@
 DN = 128
 DV = 128
 STEPS = 5
-HB = 2
+HB = 8
 TOK = 128
 N_CTX = 32
 SCALE = (DN + DR) ** -0.5
@@ -65,32 +65,42 @@
         acc[...] = jnp.zeros_like(acc)
         racc[...] = jnp.zeros_like(racc)
 
-    rot = jnp.concatenate([q[:, DN : DN + DR], q[:, 2 * DN + DR :]], 0)
+    zero = jnp.zeros((TOK, TOK), BF16)
     proj = dot_n(scaled[...], w[...]).astype(BF16)
-    srot = dot_t(rope[...], rot)
-    zero = jnp.zeros((TOK, TOK), BF16)
-    dss, dkvs = [], []
-    for i in range(HB):
-        qn = q[:, i * (DN + DR) : i * (DN + DR) + DN]
-        ct = cot[:, i * DV : (i + 1) * DV]
-        diag = jnp.concatenate(
-            [jnp.concatenate([qn, zero], 1), jnp.concatenate([zero, ct], 1)], 0
+    dkvs = []
+    rtotal = None
+    for pair in range(HB // 2):
+        base = 2 * pair * (DN + DR)
+        rot = jnp.concatenate(
+            [q[:, base + DN : base + DN + DR], q[:, base + 2 * DN + DR : base + 2 * (DN + DR)]], 0
         )
-        head = step * HB + i
-        off = offs[pl.ds(head, 1), :] * LOG2E
-        cor = corr[pl.ds(head, 1), :]
-        ph = proj[:, i * 256 : (i + 1) * 256]
-        sd = dot_t(ph, diag)
-        s = sd[:, :TOK] + srot[:, i * TOK : (i + 1) * TOK]
-        p = jnp.exp2(s * (SCALE * LOG2E) + (bias[...] - off))
-        ds = (p * (sd[:, TOK:] - cor)).astype(BF16)
-        pb = p.astype(BF16)
-        dkv = dot_n(jnp.concatenate([ds, pb], 1), diag)
-        dkvs.append((dkv * mul[...]).astype(BF16))
-        dss.append(ds)
-        kr = jnp.concatenate([ph[:, :DN], rope[...]], 1)
-        dq[:, i * (DN + DR) : (i + 1) * (DN + DR)] = (dot_l(ds, kr) * SCALE).astype(BF16)
-    racc[...] += dot_n(jnp.concatenate(dss, 1), rot)
+        srot = dot_t(rope[...], rot)
+        pp = proj[:, pair * 512 : (pair + 1) * 512]
+        dss = []
+        for j in range(2):
+            i = 2 * pair + j
+            qn = q[:, i * (DN + DR) : i * (DN + DR) + DN]
+            ct = cot[:, i * DV : (i + 1) * DV]
+            diag = jnp.concatenate(
+                [jnp.concatenate([qn, zero], 1), jnp.concatenate([zero, ct], 1)], 0
+            )
+            head = step * HB + i
+            off = offs[pl.ds(head, 1), :] * LOG2E
+            cor = corr[pl.ds(head, 1), :]
+            ph = pp[:, j * 256 : (j + 1) * 256]
+            sd = dot_t(ph, diag)
+            s = sd[:, :TOK] + srot[:, j * TOK : (j + 1) * TOK]
+            p = jnp.exp2(s * (SCALE * LOG2E) + (bias[...] - off))
+            ds = (p * (sd[:, TOK:] - cor)).astype(BF16)
+            pb = p.astype(BF16)
+            dkv = dot_n(jnp.concatenate([ds, pb], 1), diag)
+            dkvs.append((dkv * mul[...]).astype(BF16))
+            dss.append(ds)
+            kr = jnp.concatenate([ph[:, :DN], rope[...]], 1)
+            dq[:, i * (DN + DR) : (i + 1) * (DN + DR)] = (dot_l(ds, kr) * SCALE).astype(BF16)
+        rpart = dot_n(jnp.concatenate(dss, 1), rot)
+        rtotal = rpart if rtotal is None else rtotal + rpart
+    racc[...] += rtotal
     acc[...] += dot_t(jnp.concatenate(dkvs, 1), w[...])
 
     @pl.when(step == H // HB - 1)
@@ -101,8 +111,8 @@
             g = acc[part, :]
             tile = lats[i][:KVL, :].astype(F32).T
             total = total + jnp.sum(g * tile, axis=0, keepdims=True)
-            grads[i][:KVL, :] = g.T
-            grads[i][KVL:, :] = (racc[part, :] * SCALE).T
+            grads[i][:KVL, :] = g.T.astype(grads[i].dtype)
+            grads[i][KVL:, :] = (racc[part, :] * SCALE).T.astype(grads[i].dtype)
         gain_part[...] = total
 
 
@@ -117,7 +127,7 @@
         functools.partial(kernel_mul, steps),
         grid=(H // HB,),
         out_shape=[jax.ShapeDtypeStruct((TOK, H * (DN + DR)), BF16)]
-        + [jax.ShapeDtypeStruct((KVL + DR, TOK), F32)] * n
+        + [jax.ShapeDtypeStruct((KVL + DR, TOK), BF16 if s else F32) for s in steps]
         + [jax.ShapeDtypeStruct((1, KVL), F32)],
         in_specs=[sm, sm, full(1, KVL), full(H, TOK), full(H, TOK)]
         + [full(KVL + DR, TOK)] * n
@@ -148,25 +158,10 @@
     kernel(steps, *rest, mul)
 
 
-def xor_sum(x, bits):
-    parts = [x]
-    for bit in bits:
-        parts = parts + [
-            lax.ppermute(x, "ctx", [(i, i ^ (bit ^ done)) for i in range(lax.axis_size("ctx"))])
-            for done in shifts(bits, bit)
-        ]
-    while len(parts) > 1:
-        parts = [a + b for a, b in zip(parts[::2], parts[1::2])]
-    return parts[0]
-
-
-def shifts(bits, bit):
-    low = [0]
-    for other in bits:
-        if other == bit:
-            break
-        low = low + [v ^ other for v in low]
-    return low
+def everywhere_sum(row):
+    count = lax.axis_size("ctx") * lax.axis_size("dp")
+    rows = jnp.broadcast_to(row, (count, row.shape[1]))
+    return jnp.sum(lax.all_to_all(rows, ("ctx", "dp"), 0, 0, tiled=True), 0)
 
 
 def moved(x, distance):
@@ -191,9 +186,8 @@
         cotangent[0],
     )
     back = [moved(grads[s], -s) for s in range(1, STEPS)]
-    gain_sum = lax.psum(gain_part[0], "dp")
-    for bits in ((1, 2), (4,), (8, 16)):
-        gain_sum = xor_sum(gain_sum, bits)
+    gain_sum = everywhere_sum(gain_part)
+    back = [b.astype(F32) for b in back]
     total = grads[0] + ((back[0] + back[1]) + (back[2] + back[3]))
     factor = jnp.concatenate([latent_gain, jnp.ones((DR,), F32)])
     return dq[None], (total * factor[:, None]).T[None], gain_sum

time: 142 us -> 105 us (0.74)
  the two profiles are of different devices: /device:TPU:6 before, /device:TPU:1 now
where the time goes in v1:
time: 105 us
  Pallas kernels  53.5 us (51%)
  waiting for transfers between devices  23.3 us (22%)
  starting transfers between devices  22.9 us (22%)
  other arithmetic  2.61 us (2%)
  local copies, waits for them, and re-layouts  2.17 us (2%)
    pallas_call x1, Pallas kernels, visits(): pl.pallas_call(functools.partial(kernel_mul, steps), grid=(H // HB,), out...  53.5 us
    ppermute x8, starting transfers between devices, moved(): return lax.ppermute(x, 'ctx', [((i - distance) % n, i) for i in range(n)])  14.1 us
    ppermute x8, waiting for transfers between devices, moved(): return lax.ppermute(x, 'ctx', [((i - distance) % n, i) for i in range(n)])  13.7 us
    all_to_all x1, waiting for transfers between devices, everywhere_sum(): return jnp.sum(lax.all_to_all(rows, ('ctx', 'dp'), 0, 0, tiled=True), 0)  9.54 us
    all_to_all x1, starting transfers between devices, everywhere_sum(): return jnp.sum(lax.all_to_all(rows, ('ctx', 'dp'), 0, 0, tiled=True), 0)  8.85 us
  transfers between devices with their start and end apart: 9, of which 4 were waited for; matrix products, arithmetic and copies ran while one was open for 3% of the time, Pallas kernels for 0%

profile of v1, /device:TPU:1, one launch (start us, length us, event | category | flops | bytes accessed | tf_op | source)
XLA Modules:
  0.0 105.2 jit_solution(16325959083044044376)
XLA Ops:
  0.6 2.1 %collective-permute-start = (bf16[576,128]{1,0:T(8,128)(2,1)}, bf16[576,128]{1,0:T(8,128)(2,1)S(1)}, u32[]{:S(2)}, u32[]{:S(2)}) collective-permute-start(bf16[576,128]{1,0:T(8,128)(2,1)} %bitcast.17), channel_id=1, source_target_pairs={{124,0},{0,4},{4,8},{8,12},{12,16},{16,20},{20,24},{24,28},{28,32}... | collective-permute-start | bytes 442376 | tf_op jit(solution)/shard_map/ppermute | solution.py:169
  2.7 2.5 %collective-permute-start.1 = (bf16[576,128]{1,0:T(8,128)(2,1)}, bf16[576,128]{1,0:T(8,128)(2,1)S(1)}, u32[]{:S(2)}, u32[]{:S(2)}) collective-permute-start(bf16[576,128]{1,0:T(8,128)(2,1)} %bitcast.18), channel_id=1, source_target_pairs={{120,0},{124,4},{0,8},{4,12},{8,16},{12,20},{16,24},{20,28},{24,32... | collective-permute-start | bytes 442376 | tf_op jit(solution)/shard_map/ppermute | solution.py:169
  5.2 4.5 %collective-permute-start.2 = (bf16[576,128]{1,0:T(8,128)(2,1)}, bf16[576,128]{1,0:T(8,128)(2,1)S(1)}, u32[]{:S(2)}, u32[]{:S(2)}) collective-permute-start(bf16[576,128]{1,0:T(8,128)(2,1)} %bitcast.19), channel_id=1, source_target_pairs={{116,0},{120,4},{124,8},{0,12},{4,16},{8,20},{12,24},{16,28},{20,3... | collective-permute-start | bytes 442376 | tf_op jit(solution)/shard_map/ppermute | solution.py:169
  9.7 0.4 collective-permute-start.3
  10.0 3.5 %collective-permute-done.refs_6_ = bf16[576,128]{1,0:T(8,128)(2,1)S(1)} collective-permute-done((bf16[576,128]{1,0:T(8,128)(2,1)}, bf16[576,128]{1,0:T(8,128)(2,1)S(1)}, u32[]{:S(2)}, u32[]{:S(2)}) %collective-permute-start) | collective-permute-done | bytes 147488 | tf_op jit(solution)/shard_map/ppermute | solution.py:169
  13.6 0.0 copy-start
  13.6 4.9 %collective-permute-done.1.refs_7_ = bf16[576,128]{1,0:T(8,128)(2,1)S(1)} collective-permute-done((bf16[576,128]{1,0:T(8,128)(2,1)}, bf16[576,128]{1,0:T(8,128)(2,1)S(1)}, u32[]{:S(2)}, u32[]{:S(2)}) %collective-permute-start.1) | collective-permute-done | bytes 147488 | tf_op jit(solution)/shard_map/ppermute | solution.py:169
  18.4 0.0 copy-start.1
  18.4 0.0 collective-permute-done.2.refs_8_
  18.4 0.0 copy-start.2
  18.4 5.3 %collective-permute-done.3.refs_9_ = bf16[576,128]{1,0:T(8,128)(2,1)S(1)} collective-permute-done((bf16[576,128]{1,0:T(8,128)(2,1)}, bf16[576,128]{1,0:T(8,128)(2,1)S(1)}, u32[]{:S(2)}, u32[]{:S(2)}) %collective-permute-start.3) | collective-permute-done | bytes 147488 | tf_op jit(solution)/shard_map/ppermute | solution.py:169
  23.8 0.0 copy-start.3
  23.8 0.0 copy-done
  23.8 0.0 copy-done.1
  23.8 0.0 copy-done.2
  23.8 0.6 copy-done.3
  24.4 0.0 copy-start.4
  24.4 53.5 %shard_map.103 = (bf16[128,12288]{1,0:T(8,128)(2,1)}, f32[576,128]{1,0:T(8,128)}, bf16[576,128]{1,0:T(8,128)(2,1)}, bf16[576,128]{1,0:T(8,128)(2,1)}, bf16[576,1...) custom-call(s32[1,64]{1,0:T(1,128)} %refs_0_.1, s32[1]{0:T(128)} %bitcast.refs_1_, f32[1,512]{1,0:T(1,128)} %bitcast.24, ...), custom_call_target="tpu_custom_call" | custom-call | tf_op jit(solution)/shard_map/pallas_call | solution.py:126
  77.9 0.1 collective-permute-start.4
  78.0 3.2 %collective-permute-start.5 = (bf16[576,128]{1,0:T(8,128)(2,1)}, bf16[576,128]{1,0:T(8,128)(2,1)S(1)}, u32[]{:S(2)}, u32[]{:S(2)}) collective-permute-start(bf16[576,128]{1,0:T(8,128)(2,1)} %get-tuple-element.13), channel_id=1, source_target_pairs={{8,0},{12,4},{16,8},{20,12},{24,16},{28,20},{32,24},{36,28},{40,32... | collective-permute-start | bytes 442376 | tf_op jit(solution)/shard_map/ppermute | solution.py:169
  81.2 0.9 collective-permute-start.6
  82.1 0.5 collective-permute-start.7
  82.6 1.5 %broadcast_in_dim.19 = f32[128,1,512]{2,1,0:T(1,128)} broadcast(f32[512]{0:T(512)} %bitcast.25), dimensions={2} | broadcast | bytes 264192 | tf_op jit(solution)/shard_map/broadcast_in_dim | solution.py:163
  84.1 8.8 %all-to-all-start = ((f32[128,1,512]{2,1,0:T(1,128)}), f32[128,1,512]{2,1,0:T(1,128)S(1)}, u32[]{:S(2)}, u32[]{:S(2)}) async-start(f32[128,1,512]{2,1,0:T(1,128)} %broadcast_in_dim.19), calls=%async_computation | async-start | bytes 524288 | tf_op jit(solution)/shard_map/all_to_all | solution.py:164
  92.9 0.0 copy-done.4
  93.0 0.0 collective-permute-done.4
  93.0 0.0 collective-permute-done.5
  93.0 0.0 collective-permute-done.6
  93.0 0.0 collective-permute-done.7
  93.0 1.8 %multiply_bitcast_fusion = f32[1,128,576]{1,2,0:T(8,128)} fusion(f32[576,128]{1,0:T(8,128)} %get-tuple-element.11, bf16[576,128]{1,0:T(8,128)(2,1)S(1)} %collective-permute-done.7, bf16[576,128]{1,0:T(8,128)(2,1)S(1)} %collective-permute-done.6, bf16[576,128]{1,0:T(8,128)(2,1)S(1)} %collective-permute-done.5, bf16[576,128]{1,0:T(8,128)(2,1)S(1)} %collective-permute-done.4, ...), kind=kLoop, calls=%fused_computation | loop fusion | flops 663552 | bytes 1181952 | tf_op jit(solution)/shard_map/broadcast_in_dim | solution.py:193
  94.8 9.5 %all-to-all-done = f32[128,1,512]{2,1,0:T(1,128)S(1)} async-done(((f32[128,1,512]{2,1,0:T(1,128)}), f32[128,1,512]{2,1,0:T(1,128)S(1)}, u32[]{:S(2)}, u32[]{:S(2)}) %all-to-all-start) | async-done | bytes 262176 | tf_op jit(solution)/shard_map/all_to_all | solution.py:164
  104.4 0.8 reduce_sum.9
  (1 shorter events, 0.0 us)
Async XLA Ops:
  0.6 12.9 %collective-permute-start = (bf16[576,128]{1,0:T(8,128)(2,1)}, bf16[576,128]{1,0:T(8,128)(2,1)S(1)}, u32[]{:S(2)}, u32[]{:S(2)}) collective-permute-start(bf16[576,128]{1,0:T(8,128)(2,1)} %bitcast.17), channel_id=1, source_target_pairs={{124,0},{0,4},{4,8},{8,12},{12,16},{16,20},{20,24},{24,28},{28,32}... | collective-permute-start | bytes 442376 | tf_op jit(solution)/shard_map/ppermute | solution.py:169
  2.7 15.7 %collective-permute-start.1 = (bf16[576,128]{1,0:T(8,128)(2,1)}, bf16[576,128]{1,0:T(8,128)(2,1)S(1)}, u32[]{:S(2)}, u32[]{:S(2)}) collective-permute-start(bf16[576,128]{1,0:T(8,128)(2,1)} %bitcast.18), channel_id=1, source_target_pairs={{120,0},{124,4},{0,8},{4,12},{8,16},{12,20},{16,24},{20,28},{24,32... | collective-permute-start | bytes 442376 | tf_op jit(solution)/shard_map/ppermute | solution.py:169
  5.2 13.3 %collective-permute-start.2 = (bf16[576,128]{1,0:T(8,128)(2,1)}, bf16[576,128]{1,0:T(8,128)(2,1)S(1)}, u32[]{:S(2)}, u32[]{:S(2)}) collective-permute-start(bf16[576,128]{1,0:T(8,128)(2,1)} %bitcast.19), channel_id=1, source_target_pairs={{116,0},{120,4},{124,8},{0,12},{4,16},{8,20},{12,24},{16,28},{20,3... | collective-permute-start | bytes 442376 | tf_op jit(solution)/shard_map/ppermute | solution.py:169
  9.7 14.1 %collective-permute-start.3 = (bf16[576,128]{1,0:T(8,128)(2,1)}, bf16[576,128]{1,0:T(8,128)(2,1)S(1)}, u32[]{:S(2)}, u32[]{:S(2)}) collective-permute-start(bf16[576,128]{1,0:T(8,128)(2,1)} %bitcast.20), channel_id=1, source_target_pairs={{112,0},{116,4},{120,8},{124,12},{0,16},{4,20},{8,24},{12,28},{16,... | collective-permute-start | bytes 442376 | tf_op jit(solution)/shard_map/ppermute | solution.py:169
  13.6 10.2 %copy-start = (bf16[576,128]{1,0:T(8,128)(2,1)}, bf16[576,128]{1,0:T(8,128)(2,1)S(1)}, u32[]{:S(2)}) copy-start(bf16[576,128]{1,0:T(8,128)(2,1)S(1)} %collective-permute-done.refs_6_) | copy-start | bytes 442372
  18.4 5.3 %copy-start.1 = (bf16[576,128]{1,0:T(8,128)(2,1)}, bf16[576,128]{1,0:T(8,128)(2,1)S(1)}, u32[]{:S(2)}) copy-start(bf16[576,128]{1,0:T(8,128)(2,1)S(1)} %collective-permute-done.1.refs_7_) | copy-start | bytes 442372
  18.4 5.3 %copy-start.2 = (bf16[576,128]{1,0:T(8,128)(2,1)}, bf16[576,128]{1,0:T(8,128)(2,1)S(1)}, u32[]{:S(2)}) copy-start(bf16[576,128]{1,0:T(8,128)(2,1)S(1)} %collective-permute-done.2.refs_8_) | copy-start | bytes 442372
  23.8 0.6 copy-start.3
  24.4 68.5 %copy-start.4 = (f32[512]{0:T(512)S(1)}, f32[512]{0:T(512)}, u32[]{:S(2)}) copy-start(f32[512]{0:T(512)} %param.14) | copy-start | bytes 6148
  77.9 15.1 %collective-permute-start.4 = (bf16[576,128]{1,0:T(8,128)(2,1)}, bf16[576,128]{1,0:T(8,128)(2,1)S(1)}, u32[]{:S(2)}, u32[]{:S(2)}) collective-permute-start(bf16[576,128]{1,0:T(8,128)(2,1)} %get-tuple-element.12), channel_id=1, source_target_pairs={{4,0},{8,4},{12,8},{16,12},{20,16},{24,20},{28,24},{32,28},{36,32}... | collective-permute-start | bytes 442376 | tf_op jit(solution)/shard_map/ppermute | solution.py:169
  78.0 15.0 %collective-permute-start.5 = (bf16[576,128]{1,0:T(8,128)(2,1)}, bf16[576,128]{1,0:T(8,128)(2,1)S(1)}, u32[]{:S(2)}, u32[]{:S(2)}) collective-permute-start(bf16[576,128]{1,0:T(8,128)(2,1)} %get-tuple-element.13), channel_id=1, source_target_pairs={{8,0},{12,4},{16,8},{20,12},{24,16},{28,20},{32,24},{36,28},{40,32... | collective-permute-start | bytes 442376 | tf_op jit(solution)/shard_map/ppermute | solution.py:169
  81.2 11.8 %collective-permute-start.6 = (bf16[576,128]{1,0:T(8,128)(2,1)}, bf16[576,128]{1,0:T(8,128)(2,1)S(1)}, u32[]{:S(2)}, u32[]{:S(2)}) collective-permute-start(bf16[576,128]{1,0:T(8,128)(2,1)} %get-tuple-element.14), channel_id=1, source_target_pairs={{12,0},{16,4},{20,8},{24,12},{28,16},{32,20},{36,24},{40,28},{44,3... | collective-permute-start | bytes 442376 | tf_op jit(solution)/shard_map/ppermute | solution.py:169
  82.1 10.9 %collective-permute-start.7 = (bf16[576,128]{1,0:T(8,128)(2,1)}, bf16[576,128]{1,0:T(8,128)(2,1)S(1)}, u32[]{:S(2)}, u32[]{:S(2)}) collective-permute-start(bf16[576,128]{1,0:T(8,128)(2,1)} %get-tuple-element.15), channel_id=1, source_target_pairs={{16,0},{20,4},{24,8},{28,12},{32,16},{36,20},{40,24},{44,28},{48,3... | collective-permute-start | bytes 442376 | tf_op jit(solution)/shard_map/ppermute | solution.py:169
  84.1 20.3 %all-to-all-start = ((f32[128,1,512]{2,1,0:T(1,128)}), f32[128,1,512]{2,1,0:T(1,128)S(1)}, u32[]{:S(2)}, u32[]{:S(2)}) async-start(f32[128,1,512]{2,1,0:T(1,128)} %broadcast_in_dim.19), calls=%async_computation | async-start | bytes 524288 | tf_op jit(solution)/shard_map/all_to_all | solution.py:164

commit v2 on v1

v2 whole, which is shorter than its diff:
```python
import functools
import jax
import jax.numpy as jnp
from jax import lax
from jax.experimental import pallas as pl
from jax.experimental.pallas import tpu as pltpu
from jax.sharding import PartitionSpec as P

H = 64
KVL = 512
DR = 64
DN = 128
DV = 128
STEPS = 5
HB = 8
LATER = 4
TOK = 128
N_CTX = 32
SCALE = (DN + DR) ** -0.5
LOG2E = 1.4426950408889634
F32 = jnp.float32
BF16 = jnp.bfloat16


def dot_t(a, b):
    return lax.dot_general(a, b, (((1,), (1,)), ((), ())), preferred_element_type=F32)


def dot_l(a, b):
    return lax.dot_general(a, b, (((0,), (0,)), ((), ())), preferred_element_type=F32)


def dot_n(a, b):
    return jnp.dot(a, b, preferred_element_type=F32)


def copy_out(step, slot, held, stored, sem):
    return pltpu.make_async_copy(held.at[slot], stored.at[step], sem.at[slot])


def kernel(steps, order, member, gain, mul, offs, corr, *refs):
    n = len(steps)
    lats = refs[:n]
    w, q, cot, dq, stored, rope = refs[n : n + 6]
    grads = refs[n + 6 : 2 * n + 6]
    gain_rows = refs[2 * n + 6]
    scaled, bias, acc, racc, held, sem = refs[2 * n + 7 :]
    step = pl.program_id(0)
    half = TOK // 2

    @pl.when(step == 0)
    def _():
        rows = lax.broadcasted_iota(jnp.int32, (TOK, TOK), 0)
        cols = lax.broadcasted_iota(jnp.int32, (TOK, TOK), 1)
        own = member[0]

        def positions(index, group):
            block = jnp.where(index < half, order[0, 2 * group], order[0, 2 * group + 1])
            return block * half + lax.rem(index, half)

        qpos = positions(cols, own)
        for i, s in enumerate(steps):
            group = lax.rem(own + N_CTX - s, N_CTX)
            kpos = positions(rows, group)
            part = pl.ds(i * TOK, TOK)
            bias[part, :] = jnp.where(kpos <= qpos, 0.0, -1e30)
            tile = lats[i][...].astype(F32).T
            scaled[part, :] = (tile[:, :KVL] * gain[...]).astype(BF16)
            rope[part, :] = tile[:, KVL:].astype(BF16)
        acc[...] = jnp.zeros_like(acc)
        racc[...] = jnp.zeros_like(racc)

    def heads(slot):
        zero = jnp.zeros((TOK, TOK), BF16)
        proj = dot_n(scaled[...], w[...]).astype(BF16)
        dkvs = []
        rtotal = None
        for pair in range(HB // 2):
            base = 2 * pair * (DN + DR)
            rot = jnp.concatenate(
                [q[:, base + DN : base + DN + DR], q[:, base + 2 * DN + DR : base + 2 * (DN + DR)]], 0
            )
            srot = dot_t(rope[...], rot)
            dss = []
            for j in range(2):
                i = 2 * pair + j
                qn = q[:, i * (DN + DR) : i * (DN + DR) + DN]
                ct = cot[:, i * DV : (i + 1) * DV]
                diag = jnp.concatenate(
                    [jnp.concatenate([qn, zero], 1), jnp.concatenate([zero, ct], 1)], 0
                )
                head = step * HB + i
                off = offs[pl.ds(head, 1), :] * LOG2E
                cor = corr[pl.ds(head, 1), :]
                ph = proj[:, i * (DN + DV) : (i + 1) * (DN + DV)]
                sd = dot_t(ph, diag)
                s = sd[:, :TOK] + srot[:, j * TOK : (j + 1) * TOK]
                p = jnp.exp2(s * (SCALE * LOG2E) + (bias[...] - off))
                ds = (p * (sd[:, TOK:] - cor)).astype(BF16)
                pb = p.astype(BF16)
                dkv = dot_n(jnp.concatenate([ds, pb], 1), diag)
                dkvs.append((dkv * mul[...]).astype(BF16))
                dss.append(ds)
                if slot is None:
                    kr = jnp.concatenate([ph[:, :DN], rope[...]], 1)
                    dq[:, i * (DN + DR) : (i + 1) * (DN + DR)] = (dot_l(ds, kr) * SCALE).astype(BF16)
                else:
                    held[slot, 2 * i] = ds
                    held[slot, 2 * i + 1] = ph[:, :DN]
            rpart = dot_n(jnp.concatenate(dss, 1), rot)
            rtotal = rpart if rtotal is None else rtotal + rpart
        racc[...] += rtotal
        acc[...] += dot_t(jnp.concatenate(dkvs, 1), w[...])

    slot = lax.rem(step, 2)

    @pl.when(jnp.logical_and(step >= 2, step < LATER + 2))
    def _():
        copy_out(step - 2, slot, held, stored, sem).wait()

    @pl.when(step < LATER)
    def _():
        heads(slot)
        copy_out(step, slot, held, stored, sem).start()

    @pl.when(step >= LATER)
    def _():
        heads(None)

    @pl.when(step == H // HB - 1)
    def _():
        total = jnp.zeros((1, KVL), F32)
        for i in range(n):
            part = pl.ds(i * TOK, TOK)
            g = acc[part, :]
            tile = lats[i][:KVL, :].astype(F32).T
            total = total + jnp.sum(g * tile, axis=0, keepdims=True)
            grads[i][:KVL, :] = g.T.astype(grads[i].dtype)
            grads[i][KVL:, :] = (racc[part, :] * SCALE).T.astype(grads[i].dtype)
        gain_rows[...] = jnp.broadcast_to(total[None], gain_rows.shape)


def later_kernel(stored, rope, _, dq):
    for i in range(HB):
        kr = jnp.concatenate([stored[0, 2 * i + 1], rope[...]], 1)
        dq[:, i * (DN + DR) : (i + 1) * (DN + DR)] = (dot_l(stored[0, 2 * i], kr) * SCALE).astype(BF16)


def later_queries(stored, rope, dq):
    rows = stored.shape[2]
    return pl.pallas_call(
        later_kernel,
        grid=(LATER,),
        out_shape=jax.ShapeDtypeStruct(dq.shape, dq.dtype),
        in_specs=[
            pl.BlockSpec((1, 2 * HB, rows, TOK), lambda i: (i, 0, 0, 0)),
            pl.BlockSpec((rows, DR), lambda i: (0, 0)),
            pl.BlockSpec(memory_space=pl.ANY),
        ],
        out_specs=pl.BlockSpec((TOK, HB * (DN + DR)), lambda i: (0, i)),
        input_output_aliases={2: 0},
        compiler_params=pltpu.CompilerParams(vmem_limit_bytes=40 * 2**20),
        cost_estimate=pl.CostEstimate(
            flops=2 * LATER * HB * TOK * rows * (DN + DR),
            bytes_accessed=LATER * HB * TOK * (4 * rows + 2 * (DN + DR)),
            transcendentals=0,
        ),
    )(stored, rope, dq)


def visits(steps, order, member, gain, offs, corr, lats, w, q, cot, peers):
    n = len(steps)
    rows = n * TOK
    sm = pl.BlockSpec(memory_space=pltpu.SMEM)
    mul = jnp.concatenate([jnp.full((1, DN), SCALE, F32), jnp.ones((1, DV), F32)], 1)
    full = lambda *s: pl.BlockSpec(s, lambda i: (0,) * len(s))
    return pl.pallas_call(
        functools.partial(kernel, steps),
        grid=(H // HB,),
        out_shape=[
            jax.ShapeDtypeStruct((TOK, H * (DN + DR)), BF16),
            jax.ShapeDtypeStruct((LATER, 2 * HB, rows, TOK), BF16),
            jax.ShapeDtypeStruct((rows, DR), BF16),
        ]
        + [jax.ShapeDtypeStruct((KVL + DR, TOK), BF16 if s else F32) for s in steps]
        + [jax.ShapeDtypeStruct((peers, 1, KVL), F32)],
        in_specs=[sm, sm, full(1, KVL), full(1, DN + DV), full(H, TOK), full(H, TOK)]
        + [full(KVL + DR, TOK)] * n
        + [
            pl.BlockSpec((KVL, HB * (DN + DV)), lambda i: (0, i)),
            pl.BlockSpec((TOK, HB * (DN + DR)), lambda i: (0, i)),
            pl.BlockSpec((TOK, HB * DV), lambda i: (0, i)),
        ],
        out_specs=[
            pl.BlockSpec((TOK, HB * (DN + DR)), lambda i: (0, jnp.maximum(i, LATER))),
            pl.BlockSpec(memory_space=pl.ANY),
            full(rows, DR),
        ]
        + [full(KVL + DR, TOK)] * n
        + [full(peers, 1, KVL)],
        scratch_shapes=[
            pltpu.VMEM((rows, KVL), BF16),
            pltpu.VMEM((rows, TOK), F32),
            pltpu.VMEM((rows, KVL), F32),
            pltpu.VMEM((rows, DR), F32),
            pltpu.VMEM((2, 2 * HB, rows, TOK), BF16),
            pltpu.SemaphoreType.DMA((2,)),
        ],
        compiler_params=pltpu.CompilerParams(vmem_limit_bytes=60 * 2**20),
    )(order, member, gain, mul, offs, corr, *lats, w, q, cot)


def everywhere_sum(rows):
    moved_rows = lax.all_to_all(rows, ("ctx", "dp"), 0, 0, tiled=True)
    return jnp.sum(moved_rows, (0, 1))


def moved(x, distance):
    n = lax.axis_size("ctx")
    return lax.ppermute(x, "ctx", [((i - distance) % n, i) for i in range(n)])


def body(queries, latents, cotangent, offsets, corrections, span_order, latent_gain, up_weight):
    own = latents[0].T
    member = lax.axis_index("ctx").astype(jnp.int32).reshape(1)
    lats = [own] + [moved(own, s) for s in range(1, STEPS)]
    dq, stored, rope, *grads, gain_rows = visits(
        tuple(range(STEPS)),
        span_order,
        member,
        latent_gain[None],
        offsets[0],
        corrections[0],
        lats,
        up_weight,
        queries[0],
        cotangent[0],
        lax.axis_size("ctx") * lax.axis_size("dp"),
    )
    back = [moved(grads[s], -s) for s in range(1, STEPS)]
    gain_sum = everywhere_sum(gain_rows)
    dq = later_queries(stored, rope, dq)
    back = [b.astype(F32) for b in back]
    total = grads[0] + ((back[0] + back[1]) + (back[2] + back[3]))
    factor = jnp.concatenate([latent_gain, jnp.ones((DR,), F32)])
    return dq[None], (total * factor[:, None]).T[None], gain_sum


def solution(mesh):
    in_specs = (
        P("dp", "ctx", None),
        P("dp", "ctx", None),
        P("dp", "ctx", None),
        P("dp", None, "ctx"),
        P("dp", None, "ctx"),
        P("dp", None),
        P(),
        P(),
    )
    out_specs = (P("dp", "ctx", None), P("dp", "ctx", None), P())
    return jax.shard_map(body, mesh=mesh, in_specs=in_specs, out_specs=out_specs, check_vma=False)
```

time: 105 us -> 100 us (0.952)
  waiting for transfers between devices: 23.3 us -> 15.8 us
  local copies, waits for them, and re-layouts: 2.17 us -> 5.56 us
    all_to_all x1, waiting for transfers between devices: 9.54 us -> 2.04 us  [everywhere_sum(): moved_rows = lax.all_to_all(rows, ('ctx', 'dp'), 0, 0, tiled=True)]
    unnamed x10 -> x16, local copies, waits for them, and re-layouts: 0.65 us -> 5.55 us
    broadcast_in_dim x1 -> x0, local copies, waits for them, and re-layouts: 1.52 us -> none  [everywhere_sum(): rows = jnp.broadcast_to(row, (count, row.shape[1]))]
    pallas_call x1 -> x2, Pallas kernels: 53.5 us -> 53.5 us  [the longest x1 49.9 us: visits(): pl.pallas_call(functools.partial(kernel, steps), grid=(H // HB,), out_sha...]
  transfers between devices with their start and end apart: 9 -> 9, of which waited for: 4 -> 4; matrix products, arithmetic and copies ran while one was open for 3% -> 1% of each run, Pallas kernels for 0% -> 4%
where the time goes in v2:
time: 100 us
  Pallas kernels  53.5 us (54%)
  starting transfers between devices  22.9 us (23%)
  waiting for transfers between devices  15.8 us (16%)
  local copies, waits for them, and re-layouts  5.56 us (6%)
  other arithmetic  1.65 us (2%)
    pallas_call x1, Pallas kernels, visits(): pl.pallas_call(functools.partial(kernel, steps), grid=(H // HB,), out_sha...  49.9 us
    ppermute x8, starting transfers between devices, moved(): return lax.ppermute(x, 'ctx', [((i - distance) % n, i) for i in range(n)])  14.1 us
    ppermute x8, waiting for transfers between devices, moved(): return lax.ppermute(x, 'ctx', [((i - distance) % n, i) for i in range(n)])  13.7 us
    all_to_all x1, starting transfers between devices, everywhere_sum(): moved_rows = lax.all_to_all(rows, ('ctx', 'dp'), 0, 0, tiled=True)  8.84 us
    unnamed x16, local copies, waits for them, and re-layouts  5.55 us
    pallas_call x1, Pallas kernels, later_queries(): pl.pallas_call(later_kernel, grid=(LATER,), out_shape=jax.ShapeDtypeStruc...  3.6 us
    all_to_all x1, waiting for transfers between devices, everywhere_sum(): moved_rows = lax.all_to_all(rows, ('ctx', 'dp'), 0, 0, tiled=True)  2.04 us
  transfers between devices with their start and end apart: 9, of which 4 were waited for; matrix products, arithmetic and copies ran while one was open for 1% of the time, Pallas kernels for 4%

profile of v2, /device:TPU:1, one launch (start us, length us, event | category | flops | bytes accessed | tf_op | source)
XLA Modules:
  0.0 100.1 jit_solution(15417620811343899160)
XLA Ops:
  0.6 2.1 %collective-permute-start = (bf16[576,128]{1,0:T(8,128)(2,1)}, bf16[576,128]{1,0:T(8,128)(2,1)S(1)}, u32[]{:S(2)}, u32[]{:S(2)}) collective-permute-start(bf16[576,128]{1,0:T(8,128)(2,1)} %bitcast.17), channel_id=1, source_target_pairs={{124,0},{0,4},{4,8},{8,12},{12,16},{16,20},{20,24},{24,28},{28,32}... | collective-permute-start | bytes 442376 | tf_op jit(solution)/shard_map/ppermute | solution.py:220
  2.7 2.5 %collective-permute-start.1 = (bf16[576,128]{1,0:T(8,128)(2,1)}, bf16[576,128]{1,0:T(8,128)(2,1)S(1)}, u32[]{:S(2)}, u32[]{:S(2)}) collective-permute-start(bf16[576,128]{1,0:T(8,128)(2,1)} %bitcast.18), channel_id=1, source_target_pairs={{120,0},{124,4},{0,8},{4,12},{8,16},{12,20},{16,24},{20,28},{24,32... | collective-permute-start | bytes 442376 | tf_op jit(solution)/shard_map/ppermute | solution.py:220
  5.2 4.5 %collective-permute-start.2 = (bf16[576,128]{1,0:T(8,128)(2,1)}, bf16[576,128]{1,0:T(8,128)(2,1)S(1)}, u32[]{:S(2)}, u32[]{:S(2)}) collective-permute-start(bf16[576,128]{1,0:T(8,128)(2,1)} %bitcast.19), channel_id=1, source_target_pairs={{116,0},{120,4},{124,8},{0,12},{4,16},{8,20},{12,24},{16,28},{20,3... | collective-permute-start | bytes 442376 | tf_op jit(solution)/shard_map/ppermute | solution.py:220
  9.7 0.4 collective-permute-start.3
  10.0 3.5 %collective-permute-done.refs_1_ = bf16[576,128]{1,0:T(8,128)(2,1)S(1)} collective-permute-done((bf16[576,128]{1,0:T(8,128)(2,1)}, bf16[576,128]{1,0:T(8,128)(2,1)S(1)}, u32[]{:S(2)}, u32[]{:S(2)}) %collective-permute-start) | collective-permute-done | bytes 147488 | tf_op jit(solution)/shard_map/ppermute | solution.py:220
  13.6 0.0 copy-start.3
  13.6 4.9 %collective-permute-done.1.refs_2_ = bf16[576,128]{1,0:T(8,128)(2,1)S(1)} collective-permute-done((bf16[576,128]{1,0:T(8,128)(2,1)}, bf16[576,128]{1,0:T(8,128)(2,1)S(1)}, u32[]{:S(2)}, u32[]{:S(2)}) %collective-permute-start.1) | collective-permute-done | bytes 147488 | tf_op jit(solution)/shard_map/ppermute | solution.py:220
  18.4 0.0 copy-start.4
  18.4 0.0 collective-permute-done.2.refs_3_
  18.4 0.0 copy-start.5
  18.4 5.3 %collective-permute-done.3.refs_4_ = bf16[576,128]{1,0:T(8,128)(2,1)S(1)} collective-permute-done((bf16[576,128]{1,0:T(8,128)(2,1)}, bf16[576,128]{1,0:T(8,128)(2,1)S(1)}, u32[]{:S(2)}, u32[]{:S(2)}) %collective-permute-start.3) | collective-permute-done | bytes 147488 | tf_op jit(solution)/shard_map/ppermute | solution.py:220
  23.8 0.0 copy-start.6
  23.8 0.0 copy-done.3
  23.8 0.0 copy-done.4
  23.8 0.0 copy-done.5
  23.8 0.6 copy-done.6
  24.4 0.0 copy-start.7
  24.4 49.9 %shard_map.103 = (bf16[128,12288]{1,0:T(8,128)(2,1)}, bf16[4,16,640,128]{3,2,1,0:T(8,128)(2,1)}, bf16[640,64]{1,0:T(8,128)(2,1)}, f32[576,128]{1,0:T(8,128)}, bf...) custom-call(s32[1,64]{1,0:T(1,128)} %order.1, ...), custom_call_target="tpu_custom_call" | custom-call | tf_op jit(solution)/shard_map/pallas_call | solution.py:177
  74.4 0.1 collective-permute-start.4
  74.5 3.1 %collective-permute-start.5 = (bf16[576,128]{1,0:T(8,128)(2,1)}, bf16[576,128]{1,0:T(8,128)(2,1)S(1)}, u32[]{:S(2)}, u32[]{:S(2)}) collective-permute-start(bf16[576,128]{1,0:T(8,128)(2,1)} %get-tuple-element.17), channel_id=1, source_target_pairs={{8,0},{12,4},{16,8},{20,12},{24,16},{28,20},{32,24},{36,28},{40,32... | collective-permute-start | bytes 442376 | tf_op jit(solution)/shard_map/ppermute | solution.py:220
  77.6 0.9 collective-permute-start.6
  78.5 0.5 collective-permute-start.7
  79.0 0.0 copy-done.7
  79.0 8.8 %all-to-all-start = ((f32[128,1,512]{2,1,0:T(1,128)}), f32[128,1,512]{2,1,0:T(1,128)S(1)}, u32[]{:S(2)}, u32[]{:S(2)}) async-start(f32[128,1,512]{2,1,0:T(1,128)} %get-tuple-element.20), calls=%async_computation | async-start | bytes 524288 | tf_op jit(solution)/shard_map/all_to_all | solution.py:214
  87.9 0.0 copy-start
  87.9 4.0 %copy-done = bf16[4,16,640,128]{3,2,1,0:T(8,128)(2,1)S(1)} copy-done((bf16[4,16,640,128]{3,2,1,0:T(8,128)(2,1)S(1)}, bf16[4,16,640,128]{3,2,1,0:T(8,128)(2,1)}, u32[]{:S(2)}) %copy-start) | copy-done | bytes 10485784
  91.9 0.0 copy-start.1
  91.9 0.9 copy-done.1
  92.8 0.0 copy-start.2
  92.8 3.6 %shard_map.104 = bf16[128,12288]{1,0:T(8,128)(2,1)} custom-call(bf16[4,16,640,128]{3,2,1,0:T(8,128)(2,1)S(1)} %copy-done, bf16[640,64]{1,0:T(8,128)(2,1)S(1)} %copy-done.1, bf16[128,12288]{1,0:T(8,128)(2,1)} %get-tuple-element.14._), custom_call_target="tpu_custom_call", output_to_operand_aliasing={{}: (2, {})} | custom-call | flops 1006632960 | bytes 12058624 | tf_op jit(solution)/shard_map/pallas_call | solution.py:151
  96.4 0.0 collective-permute-done.4
  96.4 0.0 collective-permute-done.5
  96.4 0.0 collective-permute-done.6
  96.4 0.0 collective-permute-done.7
  96.4 0.0 copy-done.2
  96.4 0.9 multiply_bitcast_fusion
  97.3 2.0 %all-to-all-done = f32[128,1,512]{2,1,0:T(1,128)S(1)} async-done(((f32[128,1,512]{2,1,0:T(1,128)}), f32[128,1,512]{2,1,0:T(1,128)S(1)}, u32[]{:S(2)}, u32[]{:S(2)}) %all-to-all-start) | async-done | bytes 262176 | tf_op jit(solution)/shard_map/all_to_all | solution.py:214
  99.3 0.8 reduce_sum.9
  (1 shorter events, 0.0 us)
Async XLA Ops:
  0.6 12.9 %collective-permute-start = (bf16[576,128]{1,0:T(8,128)(2,1)}, bf16[576,128]{1,0:T(8,128)(2,1)S(1)}, u32[]{:S(2)}, u32[]{:S(2)}) collective-permute-start(bf16[576,128]{1,0:T(8,128)(2,1)} %bitcast.17), channel_id=1, source_target_pairs={{124,0},{0,4},{4,8},{8,12},{12,16},{16,20},{20,24},{24,28},{28,32}... | collective-permute-start | bytes 442376 | tf_op jit(solution)/shard_map/ppermute | solution.py:220
  2.7 15.7 %collective-permute-start.1 = (bf16[576,128]{1,0:T(8,128)(2,1)}, bf16[576,128]{1,0:T(8,128)(2,1)S(1)}, u32[]{:S(2)}, u32[]{:S(2)}) collective-permute-start(bf16[576,128]{1,0:T(8,128)(2,1)} %bitcast.18), channel_id=1, source_target_pairs={{120,0},{124,4},{0,8},{4,12},{8,16},{12,20},{16,24},{20,28},{24,32... | collective-permute-start | bytes 442376 | tf_op jit(solution)/shard_map/ppermute | solution.py:220
  5.2 13.3 %collective-permute-start.2 = (bf16[576,128]{1,0:T(8,128)(2,1)}, bf16[576,128]{1,0:T(8,128)(2,1)S(1)}, u32[]{:S(2)}, u32[]{:S(2)}) collective-permute-start(bf16[576,128]{1,0:T(8,128)(2,1)} %bitcast.19), channel_id=1, source_target_pairs={{116,0},{120,4},{124,8},{0,12},{4,16},{8,20},{12,24},{16,28},{20,3... | collective-permute-start | bytes 442376 | tf_op jit(solution)/shard_map/ppermute | solution.py:220
  9.7 14.1 %collective-permute-start.3 = (bf16[576,128]{1,0:T(8,128)(2,1)}, bf16[576,128]{1,0:T(8,128)(2,1)S(1)}, u32[]{:S(2)}, u32[]{:S(2)}) collective-permute-start(bf16[576,128]{1,0:T(8,128)(2,1)} %bitcast.20), channel_id=1, source_target_pairs={{112,0},{116,4},{120,8},{124,12},{0,16},{4,20},{8,24},{12,28},{16,... | collective-permute-start | bytes 442376 | tf_op jit(solution)/shard_map/ppermute | solution.py:220
  13.6 10.2 %copy-start.3 = (bf16[576,128]{1,0:T(8,128)(2,1)}, bf16[576,128]{1,0:T(8,128)(2,1)S(1)}, u32[]{:S(2)}) copy-start(bf16[576,128]{1,0:T(8,128)(2,1)S(1)} %collective-permute-done.refs_1_) | copy-start | bytes 442372
  18.4 5.3 %copy-start.4 = (bf16[576,128]{1,0:T(8,128)(2,1)}, bf16[576,128]{1,0:T(8,128)(2,1)S(1)}, u32[]{:S(2)}) copy-start(bf16[576,128]{1,0:T(8,128)(2,1)S(1)} %collective-permute-done.1.refs_2_) | copy-start | bytes 442372
  18.4 5.3 %copy-start.5 = (bf16[576,128]{1,0:T(8,128)(2,1)}, bf16[576,128]{1,0:T(8,128)(2,1)S(1)}, u32[]{:S(2)}) copy-start(bf16[576,128]{1,0:T(8,128)(2,1)S(1)} %collective-permute-done.2.refs_3_) | copy-start | bytes 442372
  23.8 0.7 copy-start.6
  24.4 54.6 %copy-start.7 = (f32[512]{0:T(512)S(1)}, f32[512]{0:T(512)}, u32[]{:S(2)}) copy-start(f32[512]{0:T(512)} %param.14) | copy-start | bytes 6148
  74.4 22.0 %collective-permute-start.4 = (bf16[576,128]{1,0:T(8,128)(2,1)}, bf16[576,128]{1,0:T(8,128)(2,1)S(1)}, u32[]{:S(2)}, u32[]{:S(2)}) collective-permute-start(bf16[576,128]{1,0:T(8,128)(2,1)} %get-tuple-element.16), channel_id=1, source_target_pairs={{4,0},{8,4},{12,8},{16,12},{20,16},{24,20},{28,24},{32,28},{36,32}... | collective-permute-start | bytes 442376 | tf_op jit(solution)/shard_map/ppermute | solution.py:220
  74.5 21.9 %collective-permute-start.5 = (bf16[576,128]{1,0:T(8,128)(2,1)}, bf16[576,128]{1,0:T(8,128)(2,1)S(1)}, u32[]{:S(2)}, u32[]{:S(2)}) collective-permute-start(bf16[576,128]{1,0:T(8,128)(2,1)} %get-tuple-element.17), channel_id=1, source_target_pairs={{8,0},{12,4},{16,8},{20,12},{24,16},{28,20},{32,24},{36,28},{40,32... | collective-permute-start | bytes 442376 | tf_op jit(solution)/shard_map/ppermute | solution.py:220
  77.6 18.8 %collective-permute-start.6 = (bf16[576,128]{1,0:T(8,128)(2,1)}, bf16[576,128]{1,0:T(8,128)(2,1)S(1)}, u32[]{:S(2)}, u32[]{:S(2)}) collective-permute-start(bf16[576,128]{1,0:T(8,128)(2,1)} %get-tuple-element.18), channel_id=1, source_target_pairs={{12,0},{16,4},{20,8},{24,12},{28,16},{32,20},{36,24},{40,28},{44,3... | collective-permute-start | bytes 442376 | tf_op jit(solution)/shard_map/ppermute | solution.py:220
  78.5 17.9 %collective-permute-start.7 = (bf16[576,128]{1,0:T(8,128)(2,1)}, bf16[576,128]{1,0:T(8,128)(2,1)S(1)}, u32[]{:S(2)}, u32[]{:S(2)}) collective-permute-start(bf16[576,128]{1,0:T(8,128)(2,1)} %get-tuple-element.19), channel_id=1, source_target_pairs={{16,0},{20,4},{24,8},{28,12},{32,16},{36,20},{40,24},{44,28},{48,3... | collective-permute-start | bytes 442376 | tf_op jit(solution)/shard_map/ppermute | solution.py:220
  79.0 20.3 %all-to-all-start = ((f32[128,1,512]{2,1,0:T(1,128)}), f32[128,1,512]{2,1,0:T(1,128)S(1)}, u32[]{:S(2)}, u32[]{:S(2)}) async-start(f32[128,1,512]{2,1,0:T(1,128)} %get-tuple-element.20), calls=%async_computation | async-start | bytes 524288 | tf_op jit(solution)/shard_map/all_to_all | solution.py:214
  87.9 4.0 %copy-start = (bf16[4,16,640,128]{3,2,1,0:T(8,128)(2,1)S(1)}, bf16[4,16,640,128]{3,2,1,0:T(8,128)(2,1)}, u32[]{:S(2)}) copy-start(bf16[4,16,640,128]{3,2,1,0:T(8,128)(2,1)} %get-tuple-element.12.stored) | copy-start | bytes 31457284
  91.9 0.9 copy-start.1
  92.8 3.6 %copy-start.2 = (f32[576,128]{1,0:T(8,128)S(1)}, f32[576,128]{1,0:T(8,128)}, u32[]{:S(2)}) copy-start(f32[576,128]{1,0:T(8,128)} %get-tuple-element.15) | copy-start | bytes 884740

commit v3 on v1

v3 whole, which is shorter than its diff:
```python
import functools
import jax
import jax.numpy as jnp
from jax import lax
from jax.experimental import pallas as pl
from jax.experimental.pallas import tpu as pltpu
from jax.sharding import PartitionSpec as P

H = 64
KVL = 512
DR = 64
DN = 128
DV = 128
STEPS = 5
HB = 8
LATER = 6
EARLY = 3
TOK = 128
N_CTX = 32
SCALE = (DN + DR) ** -0.5
LOG2E = 1.4426950408889634
F32 = jnp.float32
BF16 = jnp.bfloat16


def dot_t(a, b):
    return lax.dot_general(a, b, (((1,), (1,)), ((), ())), preferred_element_type=F32)


def dot_l(a, b):
    return lax.dot_general(a, b, (((0,), (0,)), ((), ())), preferred_element_type=F32)


def dot_n(a, b):
    return jnp.dot(a, b, preferred_element_type=F32)


def arrange(steps, order, member, gain, lats, scaled, rope, bias):
    half = TOK // 2
    rows = lax.broadcasted_iota(jnp.int32, (TOK, TOK), 0)
    cols = lax.broadcasted_iota(jnp.int32, (TOK, TOK), 1)
    own = member[0]

    def positions(index, group):
        block = jnp.where(index < half, order[0, 2 * group], order[0, 2 * group + 1])
        return block * half + lax.rem(index, half)

    qpos = positions(cols, own)
    for i, s in enumerate(steps):
        group = lax.rem(own + N_CTX - s, N_CTX)
        kpos = positions(rows, group)
        part = pl.ds(i * TOK, TOK)
        bias[part, :] = jnp.where(kpos <= qpos, 0.0, -1e30)
        tile = lats[i][...].astype(F32).T
        scaled[part, :] = (tile[:, :KVL] * gain[...]).astype(BF16)
        rope[part, :] = tile[:, KVL:].astype(BF16)


def heads(step, part, refs, keep, dq):
    mul, offs, corr, w, q, cot, scaled, rope, bias, acc, racc = refs
    zero = jnp.zeros((TOK, TOK), BF16)
    proj = dot_n(scaled[part, :], w[...]).astype(BF16)
    dkvs = []
    rtotal = None
    for pair in range(HB // 2):
        base = 2 * pair * (DN + DR)
        rot = jnp.concatenate(
            [q[:, base + DN : base + DN + DR], q[:, base + 2 * DN + DR : base + 2 * (DN + DR)]], 0
        )
        srot = dot_t(rope[part, :], rot)
        dss = []
        for j in range(2):
            i = 2 * pair + j
            qn = q[:, i * (DN + DR) : i * (DN + DR) + DN]
            ct = cot[:, i * DV : (i + 1) * DV]
            diag = jnp.concatenate(
                [jnp.concatenate([qn, zero], 1), jnp.concatenate([zero, ct], 1)], 0
            )
            head = step * HB + i
            off = offs[pl.ds(head, 1), :] * LOG2E
            cor = corr[pl.ds(head, 1), :]
            ph = proj[:, i * (DN + DV) : (i + 1) * (DN + DV)]
            sd = dot_t(ph, diag)
            s = sd[:, :TOK] + srot[:, j * TOK : (j + 1) * TOK]
            p = jnp.exp2(s * (SCALE * LOG2E) + (bias[part, :] - off))
            ds = (p * (sd[:, TOK:] - cor)).astype(BF16)
            pb = p.astype(BF16)
            dkv = dot_n(jnp.concatenate([ds, pb], 1), diag)
            dkvs.append((dkv * mul[...]).astype(BF16))
            dss.append(ds)
            if keep is None:
                kr = jnp.concatenate([ph[:, :DN], rope[part, :]], 1)
                dq[:, i * (DN + DR) : (i + 1) * (DN + DR)] = (dot_l(ds, kr) * SCALE).astype(BF16)
            else:
                keep(2 * i, ds)
                keep(2 * i + 1, ph[:, :DN])
        rpart = dot_n(jnp.concatenate(dss, 1), rot)
        rtotal = rpart if rtotal is None else rtotal + rpart
    racc[part, :] += rtotal
    acc[part, :] += dot_t(jnp.concatenate(dkvs, 1), w[...])


def early_kernel(
    order, member, gain, mul, offs, corr, lat, w, q, cot, stored, acc, racc, scaled, rope, bias
):
    step = pl.program_id(0)

    @pl.when(step == 0)
    def _():
        arrange((0,), order, member, gain, [lat], scaled, rope, bias)
        acc[...] = jnp.zeros_like(acc)
        racc[...] = jnp.zeros_like(racc)

    def keep(at, value):
        stored[0, at] = value

    refs = (mul, offs, corr, w, q, cot, scaled, rope, bias, acc, racc)
    heads(step, pl.ds(0, TOK), refs, keep, None)


def copy_out(step, slot, first, held, stored, sem):
    part = pl.ds(first, held.shape[2] - first)
    return pltpu.make_async_copy(
        held.at[slot, :, part], stored.at[step, :, part], sem.at[slot]
    )


def kernel(steps, order, member, gain, mul, offs, corr, *refs):
    n = len(steps)
    lats = refs[:n]
    w, q, cot, own_acc, own_racc, _, dq, stored, rope = refs[n : n + 9]
    grads = refs[n + 9 : 2 * n + 9]
    gain_rows = refs[2 * n + 9]
    scaled, bias, acc, racc, held, sem = refs[2 * n + 10 :]
    step = pl.program_id(0)
    rows = n * TOK

    @pl.when(step == 0)
    def _():
        arrange(steps, order, member, gain, lats, scaled, rope, bias)
        acc[...] = jnp.zeros_like(acc)
        racc[...] = jnp.zeros_like(racc)
        acc[pl.ds(0, TOK), :] = own_acc[...]
        racc[pl.ds(0, TOK), :] = own_racc[...]

    slot = lax.rem(step, 2)
    visitors, everyone = pl.ds(TOK, rows - TOK), pl.ds(0, rows)
    refs = (mul, offs, corr, w, q, cot, scaled, rope, bias, acc, racc)

    @pl.when(jnp.logical_and(step >= 2, step < EARLY + 2))
    def _():
        copy_out(step - 2, slot, TOK, held, stored, sem).wait()

    @pl.when(jnp.logical_and(step >= EARLY + 2, step < LATER + 2))
    def _():
        copy_out(step - 2, slot, 0, held, stored, sem).wait()

    def kept(part):
        def keep(at, value):
            held[slot, at, part, :] = value

        return keep

    @pl.when(step < EARLY)
    def _():
        heads(step, visitors, refs, kept(visitors), None)
        copy_out(step, slot, TOK, held, stored, sem).start()

    @pl.when(jnp.logical_and(step >= EARLY, step < LATER))
    def _():
        heads(step, everyone, refs, kept(everyone), None)
        copy_out(step, slot, 0, held, stored, sem).start()

    @pl.when(step >= LATER)
    def _():
        heads(step, everyone, refs, None, dq)

    @pl.when(step == H // HB - 1)
    def _():
        total = jnp.zeros((1, KVL), F32)
        for i in range(n):
            part = pl.ds(i * TOK, TOK)
            g = acc[part, :]
            tile = lats[i][:KVL, :].astype(F32).T
            total = total + jnp.sum(g * tile, axis=0, keepdims=True)
            grads[i][:KVL, :] = g.T.astype(grads[i].dtype)
            grads[i][KVL:, :] = (racc[part, :] * SCALE).T.astype(grads[i].dtype)
        gain_rows[...] = jnp.broadcast_to(total[None], gain_rows.shape)


def later_kernel(stored, rope, _, dq):
    for i in range(HB):
        kr = jnp.concatenate([stored[0, 2 * i + 1], rope[...]], 1)
        dq[:, i * (DN + DR) : (i + 1) * (DN + DR)] = (dot_l(stored[0, 2 * i], kr) * SCALE).astype(BF16)


def in_vmem(x):
    return pltpu.with_memory_space_constraint(x, pltpu.VMEM)


def later_queries(stored, rope, dq):
    rows = stored.shape[2]
    return pl.pallas_call(
        later_kernel,
        grid=(LATER,),
        out_shape=jax.ShapeDtypeStruct(dq.shape, dq.dtype),
        in_specs=[
            pl.BlockSpec((1, 2 * HB, rows, TOK), lambda i: (i, 0, 0, 0)),
            pl.BlockSpec((rows, DR), lambda i: (0, 0)),
            pl.BlockSpec(memory_space=pl.ANY),
        ],
        out_specs=pl.BlockSpec((TOK, HB * (DN + DR)), lambda i: (0, i)),
        input_output_aliases={2: 0},
        compiler_params=pltpu.CompilerParams(vmem_limit_bytes=56 * 2**20),
        cost_estimate=pl.CostEstimate(
            flops=2 * LATER * HB * TOK * rows * (DN + DR),
            bytes_accessed=LATER * HB * TOK * (4 * rows + 2 * (DN + DR)),
            transcendentals=0,
        ),
    )(stored, in_vmem(rope), dq)


def whole(*shape):
    return pl.BlockSpec(shape, lambda i: (0,) * len(shape))


def inputs_specs(n):
    sm = pl.BlockSpec(memory_space=pltpu.SMEM)
    return (
        [sm, sm, whole(1, KVL), whole(1, DN + DV), whole(H, TOK), whole(H, TOK)]
        + [whole(KVL + DR, TOK)] * n
        + [
            pl.BlockSpec((KVL, HB * (DN + DV)), lambda i: (0, i)),
            pl.BlockSpec((TOK, HB * (DN + DR)), lambda i: (0, i)),
            pl.BlockSpec((TOK, HB * DV), lambda i: (0, i)),
        ]
    )


def work(grid, rows):
    per_head = rows * (4 * KVL * (DN + DV) + 10 * TOK * DN)
    return pl.CostEstimate(
        flops=grid * HB * per_head,
        bytes_accessed=grid * HB * (2 * KVL * (DN + DV) + TOK * (4 * DN + 4 * DR)),
        transcendentals=grid * HB * rows * TOK,
    )


def early_visit(common, lat, streams):
    return pl.pallas_call(
        early_kernel,
        grid=(EARLY,),
        out_shape=[
            jax.ShapeDtypeStruct((LATER, 2 * HB, STEPS * TOK, TOK), BF16),
            pltpu.VMEM((TOK, KVL), F32),
            pltpu.VMEM((TOK, DR), F32),
        ],
        in_specs=inputs_specs(1),
        out_specs=[
            pl.BlockSpec((1, 2 * HB, TOK, TOK), lambda i: (i, 0, 0, 0)),
            whole(TOK, KVL),
            whole(TOK, DR),
        ],
        scratch_shapes=[
            pltpu.VMEM((TOK, KVL), BF16),
            pltpu.VMEM((TOK, DR), BF16),
            pltpu.VMEM((TOK, TOK), F32),
        ],
        compiler_params=pltpu.CompilerParams(vmem_limit_bytes=56 * 2**20),
        cost_estimate=work(EARLY, TOK),
    )(*common, lat, *streams)


def visits(steps, common, lats, streams, early, peers):
    n = len(steps)
    rows = n * TOK
    anywhere = pl.BlockSpec(memory_space=pl.ANY)
    stored, own_acc, own_racc = early
    return pl.pallas_call(
        functools.partial(kernel, steps),
        grid=(H // HB,),
        out_shape=[
            jax.ShapeDtypeStruct((TOK, H * (DN + DR)), BF16),
            jax.ShapeDtypeStruct(stored.shape, BF16),
            pltpu.VMEM((rows, DR), BF16),
        ]
        + [jax.ShapeDtypeStruct((KVL + DR, TOK), F32)]
        + [pltpu.VMEM((KVL + DR, TOK), BF16)] * (n - 1)
        + [jax.ShapeDtypeStruct((peers, 1, KVL), F32)],
        in_specs=inputs_specs(n) + [whole(TOK, KVL), whole(TOK, DR), anywhere],
        out_specs=[
            pl.BlockSpec((TOK, HB * (DN + DR)), lambda i: (0, jnp.maximum(i, LATER))),
            anywhere,
            whole(rows, DR),
        ]
        + [whole(KVL + DR, TOK)] * n
        + [whole(peers, 1, KVL)],
        scratch_shapes=[
            pltpu.VMEM((rows, KVL), BF16),
            pltpu.VMEM((rows, TOK), F32),
            pltpu.VMEM((rows, KVL), F32),
            pltpu.VMEM((rows, DR), F32),
            pltpu.VMEM((2, 2 * HB, rows, TOK), BF16),
            pltpu.SemaphoreType.DMA((2,)),
        ],
        input_output_aliases={6 + n + 5: 1},
        compiler_params=pltpu.CompilerParams(vmem_limit_bytes=56 * 2**20),
        cost_estimate=work(H // HB, rows),
    )(
        *common,
        lats[0],
        *map(in_vmem, lats[1:]),
        *streams,
        in_vmem(own_acc),
        in_vmem(own_racc),
        stored,
    )


def everywhere_sum(rows):
    moved_rows = lax.all_to_all(rows, ("ctx", "dp"), 0, 0, tiled=True)
    return jnp.sum(moved_rows, (0, 1))


def moved(x, distance):
    n = lax.axis_size("ctx")
    return lax.ppermute(x, "ctx", [((i - distance) % n, i) for i in range(n)])


def body(queries, latents, cotangent, offsets, corrections, span_order, latent_gain, up_weight):
    own = latents[0].T
    member = lax.axis_index("ctx").astype(jnp.int32).reshape(1)
    lats = [own] + [moved(own, s) for s in range(1, STEPS)]
    mul = jnp.concatenate([jnp.full((1, DN), SCALE, F32), jnp.ones((1, DV), F32)], 1)
    common = (span_order, member, latent_gain[None], mul, offsets[0], corrections[0])
    streams = (up_weight, queries[0], cotangent[0])
    early = early_visit(common, own, streams)
    peers = lax.axis_size("ctx") * lax.axis_size("dp")
    dq, stored, rope, *grads, gain_rows = visits(
        tuple(range(STEPS)), common, lats, streams, early, peers
    )
    back = [moved(grads[s], -s) for s in range(1, STEPS)]
    gain_sum = everywhere_sum(gain_rows)
    dq = later_queries(stored, rope, dq)
    back = [b.astype(F32) for b in back]
    total = grads[0] + ((back[0] + back[1]) + (back[2] + back[3]))
    factor = jnp.concatenate([latent_gain, jnp.ones((DR,), F32)])
    return dq[None], (total * factor[:, None]).T[None], gain_sum


def solution(mesh):
    in_specs = (
        P("dp", "ctx", None),
        P("dp", "ctx", None),
        P("dp", "ctx", None),
        P("dp", None, "ctx"),
        P("dp", None, "ctx"),
        P("dp", None),
        P(),
        P(),
    )
    out_specs = (P("dp", "ctx", None), P("dp", "ctx", None), P())
    return jax.shard_map(body, mesh=mesh, in_specs=in_specs, out_specs=out_specs, check_vma=False)
```

time: 105 us -> 96 us (0.914)
  waiting for transfers between devices: 23.3 us -> 3.74 us
  Pallas kernels: 53.5 us -> 65.2 us
  local copies, waits for them, and re-layouts: 2.17 us -> 0.01 us
  starting transfers between devices: 22.9 us -> 24.5 us
    pallas_call x1 -> x3, Pallas kernels: 53.5 us -> 65.2 us  [the longest x1 44.7 us: visits(): pl.pallas_call(functools.partial(kernel, steps), grid=(H // HB,), out_sha...]
    ppermute x8, waiting for transfers between devices: 13.7 us -> 2.87 us  [moved(): return lax.ppermute(x, 'ctx', [((i - distance) % n, i) for i in range(n)])]
    all_to_all x1, waiting for transfers between devices: 9.54 us -> 0.87 us  [everywhere_sum(): moved_rows = lax.all_to_all(rows, ('ctx', 'dp'), 0, 0, tiled=True)]
    ppermute x8, starting transfers between devices: 14.1 us -> 16 us  [moved(): return lax.ppermute(x, 'ctx', [((i - distance) % n, i) for i in range(n)])]
    broadcast_in_dim x1 -> x0, local copies, waits for them, and re-layouts: 1.52 us -> none  [everywhere_sum(): rows = jnp.broadcast_to(row, (count, row.shape[1]))]
  transfers between devices with their start and end apart: 9 -> 9, of which waited for: 4 -> 2; matrix products, arithmetic and copies ran while one was open for 3% -> 1% of each run, Pallas kernels for 0% -> 21%
where the time goes in v3:
time: 96 us; the launch traced here: 95.7 us
  Pallas kernels  65.2 us (68%)
  starting transfers between devices  24.5 us (26%)
  waiting for transfers between devices  3.74 us (4%)
  other arithmetic  1.65 us (2%)
    pallas_call x1, Pallas kernels, visits(): pl.pallas_call(functools.partial(kernel, steps), grid=(H // HB,), out_sha...  44.7 us
    ppermute x8, starting transfers between devices, moved(): return lax.ppermute(x, 'ctx', [((i - distance) % n, i) for i in range(n)])  16 us
    pallas_call x1, Pallas kernels, early_visit(): pl.pallas_call(early_kernel, grid=(EARLY,), out_shape=[jax.ShapeDtypeStru...  10.9 us
    pallas_call x1, Pallas kernels, later_queries(): pl.pallas_call(later_kernel, grid=(LATER,), out_shape=jax.ShapeDtypeStruc...  9.63 us
    all_to_all x1, starting transfers between devices, everywhere_sum(): moved_rows = lax.all_to_all(rows, ('ctx', 'dp'), 0, 0, tiled=True)  8.47 us
    ppermute x8, waiting for transfers between devices, moved(): return lax.ppermute(x, 'ctx', [((i - distance) % n, i) for i in range(n)])  2.87 us
  transfers between devices with their start and end apart: 9, of which 2 were waited for; matrix products, arithmetic and copies ran while one was open for 1% of the time, Pallas kernels for 21%

profile of v3, /device:TPU:1, one launch (start us, length us, event | category | flops | bytes accessed | tf_op | source)
XLA Modules:
  0.0 95.7 jit_solution(15424930210730366143)
XLA Ops:
  0.6 2.1 %collective-permute-start = (bf16[576,128]{1,0:T(8,128)(2,1)}, bf16[576,128]{1,0:T(8,128)(2,1)S(1)}, u32[]{:S(2)}, u32[]{:S(2)}) collective-permute-start(bf16[576,128]{1,0:T(8,128)(2,1)} %bitcast.19), channel_id=1, source_target_pairs={{124,0},{0,4},{4,8},{8,12},{12,16},{16,20},{20,24},{24,28},{28,32}... | collective-permute-start | bytes 442376 | tf_op jit(solution)/shard_map/ppermute | solution.py:327
  2.7 2.5 %collective-permute-start.1 = (bf16[576,128]{1,0:T(8,128)(2,1)}, bf16[576,128]{1,0:T(8,128)(2,1)S(1)}, u32[]{:S(2)}, u32[]{:S(2)}) collective-permute-start(bf16[576,128]{1,0:T(8,128)(2,1)} %bitcast.20), channel_id=1, source_target_pairs={{120,0},{124,4},{0,8},{4,12},{8,16},{12,20},{16,24},{20,28},{24,32... | collective-permute-start | bytes 442376 | tf_op jit(solution)/shard_map/ppermute | solution.py:327
  5.2 4.5 %collective-permute-start.2 = (bf16[576,128]{1,0:T(8,128)(2,1)}, bf16[576,128]{1,0:T(8,128)(2,1)S(1)}, u32[]{:S(2)}, u32[]{:S(2)}) collective-permute-start(bf16[576,128]{1,0:T(8,128)(2,1)} %bitcast.21), channel_id=1, source_target_pairs={{116,0},{120,4},{124,8},{0,12},{4,16},{8,20},{12,24},{16,28},{20,3... | collective-permute-start | bytes 442376 | tf_op jit(solution)/shard_map/ppermute | solution.py:327
  9.7 0.4 collective-permute-start.3
  10.0 10.9 %shard_map.103 = (bf16[6,16,640,128]{3,2,1,0:T(8,128)(2,1)}, f32[128,512]{1,0:T(8,128)S(1)}, f32[128,64]{1,0:T(8,128)S(1)}) custom-call(s32[1,64]{1,0:T(1,128)} %order.3, s32[1]{0:T(128)} %bitcast.member, f32[1,512]{1,0:T(1,128)} %bitcast.29, f32[1,256]{1,0:T(1,128)} %constant.4.clone.1.mul, f32[64,128]{1,0:T(8,128)} %bitcast.25, f32[64,128]{1,0:T(8,128)} %bitcast.27, ...), custom_call_target="tpu_custom_call" | custom-call | flops 2113929216 | bytes 8650752 | tf_op jit(solution)/shard_map/pallas_call | solution.py:250
  20.9 0.0 collective-permute-done.refs_1_
  20.9 0.0 collective-permute-done.1.refs_2_
  20.9 0.0 collective-permute-done.2.refs_3_
  20.9 2.9 %collective-permute-done.3.refs_4_ = bf16[576,128]{1,0:T(8,128)(2,1)S(1)} collective-permute-done((bf16[576,128]{1,0:T(8,128)(2,1)}, bf16[576,128]{1,0:T(8,128)(2,1)S(1)}, u32[]{:S(2)}, u32[]{:S(2)}) %collective-permute-start.3) | collective-permute-done | bytes 147488 | tf_op jit(solution)/shard_map/ppermute | solution.py:327
  23.8 0.0 copy-start.1
  23.8 44.7 %shard_map.104 = (bf16[128,12288]{1,0:T(8,128)(2,1)}, bf16[6,16,640,128]{3,2,1,0:T(8,128)(2,1)}, bf16[640,64]{1,0:T(8,128)(2,1)S(1)}, f32[576,128]{1,0:T(8,128)}...) custom-call(s32[1,64]{1,0:T(1,128)} %order.3, ...), custom_call_target="tpu_custom_call", output_to_operand_aliasing={{1}: (16, {})} | custom-call | flops 28185722880 | bytes 23068672 | tf_op jit(solution)/shard_map/pallas_call | solution.py:279
  68.5 1.7 %collective-permute-start.4 = (bf16[576,128]{1,0:T(8,128)(2,1)S(1)}, bf16[576,128]{1,0:T(8,128)(2,1)S(1)}, u32[]{:S(2)}, u32[]{:S(2)}) collective-permute-start(bf16[576,128]{1,0:T(8,128)(2,1)S(1)} %get-tuple-element.22), channel_id=1, source_target_pairs={{4,0},{8,4},{12,8},{16,12},{20,16},{24,20},{28,24},{32,28},{36,32}... | collective-permute-start | bytes 442376 | tf_op jit(solution)/shard_map/ppermute | solution.py:327
  70.2 2.1 %collective-permute-start.5 = (bf16[576,128]{1,0:T(8,128)(2,1)S(1)}, bf16[576,128]{1,0:T(8,128)(2,1)S(1)}, u32[]{:S(2)}, u32[]{:S(2)}) collective-permute-start(bf16[576,128]{1,0:T(8,128)(2,1)S(1)} %get-tuple-element.23), channel_id=1, source_target_pairs={{8,0},{12,4},{16,8},{20,12},{24,16},{28,20},{32,24},{36,28},{40,32... | collective-permute-start | bytes 442376 | tf_op jit(solution)/shard_map/ppermute | solution.py:327
  72.3 1.4 %collective-permute-start.6 = (bf16[576,128]{1,0:T(8,128)(2,1)S(1)}, bf16[576,128]{1,0:T(8,128)(2,1)S(1)}, u32[]{:S(2)}, u32[]{:S(2)}) collective-permute-start(bf16[576,128]{1,0:T(8,128)(2,1)S(1)} %get-tuple-element.24), channel_id=1, source_target_pairs={{12,0},{16,4},{20,8},{24,12},{28,16},{32,20},{36,24},{40,28},{44,3... | collective-permute-start | bytes 442376 | tf_op jit(solution)/shard_map/ppermute | solution.py:327
  73.7 1.4 %collective-permute-start.7 = (bf16[576,128]{1,0:T(8,128)(2,1)S(1)}, bf16[576,128]{1,0:T(8,128)(2,1)S(1)}, u32[]{:S(2)}, u32[]{:S(2)}) collective-permute-start(bf16[576,128]{1,0:T(8,128)(2,1)S(1)} %get-tuple-element.25), channel_id=1, source_target_pairs={{16,0},{20,4},{24,8},{28,12},{32,16},{36,20},{40,24},{44,28},{48,3... | collective-permute-start | bytes 442376 | tf_op jit(solution)/shard_map/ppermute | solution.py:327
  75.1 0.0 copy-done.1
  75.1 8.5 %all-to-all-start = ((f32[128,1,512]{2,1,0:T(1,128)}), f32[128,1,512]{2,1,0:T(1,128)S(1)}, u32[]{:S(2)}, u32[]{:S(2)}) async-start(f32[128,1,512]{2,1,0:T(1,128)} %get-tuple-element.26), calls=%async_computation | async-start | bytes 524288 | tf_op jit(solution)/shard_map/all_to_all | solution.py:321
  83.6 0.0 copy-start
  83.6 9.6 %shard_map.105 = bf16[128,12288]{1,0:T(8,128)(2,1)} custom-call(bf16[6,16,640,128]{3,2,1,0:T(8,128)(2,1)} %get-tuple-element.18.stored, bf16[640,64]{1,0:T(8,128)(2,1)S(1)} %get-tuple-element.19.rope, bf16[128,12288]{1,0:T(8,128)(2,1)} %get-tuple-element.20._), custom_call_target="tpu_custom_call", output_to_operand_aliasing={{}: (2, {})} | custom-call | flops 1509949440 | bytes 18087936 | tf_op jit(solution)/shard_map/pallas_call | solution.py:203
  93.2 0.0 collective-permute-done.4
  93.2 0.0 collective-permute-done.5
  93.2 0.0 collective-permute-done.6
  93.2 0.0 collective-permute-done.7
  93.2 0.0 copy-done
  93.2 0.9 multiply_bitcast_fusion
  94.1 0.9 all-to-all-done
  95.0 0.8 reduce_sum.9
  (1 shorter events, 0.0 us)
Async XLA Ops:
  0.6 20.3 %collective-permute-start = (bf16[576,128]{1,0:T(8,128)(2,1)}, bf16[576,128]{1,0:T(8,128)(2,1)S(1)}, u32[]{:S(2)}, u32[]{:S(2)}) collective-permute-start(bf16[576,128]{1,0:T(8,128)(2,1)} %bitcast.19), channel_id=1, source_target_pairs={{124,0},{0,4},{4,8},{8,12},{12,16},{16,20},{20,24},{24,28},{28,32}... | collective-permute-start | bytes 442376 | tf_op jit(solution)/shard_map/ppermute | solution.py:327
  2.7 18.2 %collective-permute-start.1 = (bf16[576,128]{1,0:T(8,128)(2,1)}, bf16[576,128]{1,0:T(8,128)(2,1)S(1)}, u32[]{:S(2)}, u32[]{:S(2)}) collective-permute-start(bf16[576,128]{1,0:T(8,128)(2,1)} %bitcast.20), channel_id=1, source_target_pairs={{120,0},{124,4},{0,8},{4,12},{8,16},{12,20},{16,24},{20,28},{24,32... | collective-permute-start | bytes 442376 | tf_op jit(solution)/shard_map/ppermute | solution.py:327
  5.2 15.7 %collective-permute-start.2 = (bf16[576,128]{1,0:T(8,128)(2,1)}, bf16[576,128]{1,0:T(8,128)(2,1)S(1)}, u32[]{:S(2)}, u32[]{:S(2)}) collective-permute-start(bf16[576,128]{1,0:T(8,128)(2,1)} %bitcast.21), channel_id=1, source_target_pairs={{116,0},{120,4},{124,8},{0,12},{4,16},{8,20},{12,24},{16,28},{20,3... | collective-permute-start | bytes 442376 | tf_op jit(solution)/shard_map/ppermute | solution.py:327
  9.7 14.1 %collective-permute-start.3 = (bf16[576,128]{1,0:T(8,128)(2,1)}, bf16[576,128]{1,0:T(8,128)(2,1)S(1)}, u32[]{:S(2)}, u32[]{:S(2)}) collective-permute-start(bf16[576,128]{1,0:T(8,128)(2,1)} %bitcast.22), channel_id=1, source_target_pairs={{112,0},{116,4},{120,8},{124,12},{0,16},{4,20},{8,24},{12,28},{16,... | collective-permute-start | bytes 442376 | tf_op jit(solution)/shard_map/ppermute | solution.py:327
  23.8 51.3 %copy-start.1 = (f32[512]{0:T(512)S(1)}, f32[512]{0:T(512)}, u32[]{:S(2)}) copy-start(f32[512]{0:T(512)} %param.14) | copy-start | bytes 6148
  68.5 24.7 %collective-permute-start.4 = (bf16[576,128]{1,0:T(8,128)(2,1)S(1)}, bf16[576,128]{1,0:T(8,128)(2,1)S(1)}, u32[]{:S(2)}, u32[]{:S(2)}) collective-permute-start(bf16[576,128]{1,0:T(8,128)(2,1)S(1)} %get-tuple-element.22), channel_id=1, source_target_pairs={{4,0},{8,4},{12,8},{16,12},{20,16},{24,20},{28,24},{32,28},{36,32}... | collective-permute-start | bytes 442376 | tf_op jit(solution)/shard_map/ppermute | solution.py:327
  70.2 23.0 %collective-permute-start.5 = (bf16[576,128]{1,0:T(8,128)(2,1)S(1)}, bf16[576,128]{1,0:T(8,128)(2,1)S(1)}, u32[]{:S(2)}, u32[]{:S(2)}) collective-permute-start(bf16[576,128]{1,0:T(8,128)(2,1)S(1)} %get-tuple-element.23), channel_id=1, source_target_pairs={{8,0},{12,4},{16,8},{20,12},{24,16},{28,20},{32,24},{36,28},{40,32... | collective-permute-start | bytes 442376 | tf_op jit(solution)/shard_map/ppermute | solution.py:327
  72.3 20.9 %collective-permute-start.6 = (bf16[576,128]{1,0:T(8,128)(2,1)S(1)}, bf16[576,128]{1,0:T(8,128)(2,1)S(1)}, u32[]{:S(2)}, u32[]{:S(2)}) collective-permute-start(bf16[576,128]{1,0:T(8,128)(2,1)S(1)} %get-tuple-element.24), channel_id=1, source_target_pairs={{12,0},{16,4},{20,8},{24,12},{28,16},{32,20},{36,24},{40,28},{44,3... | collective-permute-start | bytes 442376 | tf_op jit(solution)/shard_map/ppermute | solution.py:327
  73.7 19.5 %collective-permute-start.7 = (bf16[576,128]{1,0:T(8,128)(2,1)S(1)}, bf16[576,128]{1,0:T(8,128)(2,1)S(1)}, u32[]{:S(2)}, u32[]{:S(2)}) collective-permute-start(bf16[576,128]{1,0:T(8,128)(2,1)S(1)} %get-tuple-element.25), channel_id=1, source_target_pairs={{16,0},{20,4},{24,8},{28,12},{32,16},{36,20},{40,24},{44,28},{48,3... | collective-permute-start | bytes 442376 | tf_op jit(solution)/shard_map/ppermute | solution.py:327
  75.1 19.9 %all-to-all-start = ((f32[128,1,512]{2,1,0:T(1,128)}), f32[128,1,512]{2,1,0:T(1,128)S(1)}, u32[]{:S(2)}, u32[]{:S(2)}) async-start(f32[128,1,512]{2,1,0:T(1,128)} %get-tuple-element.26), calls=%async_computation | async-start | bytes 524288 | tf_op jit(solution)/shard_map/all_to_all | solution.py:321
  83.6 9.7 %copy-start = (f32[576,128]{1,0:T(8,128)S(1)}, f32[576,128]{1,0:T(8,128)}, u32[]{:S(2)}) copy-start(f32[576,128]{1,0:T(8,128)} %get-tuple-element.21) | copy-start | bytes 884740

commit v4 on v3

--- a/solution.py
+++ b/solution.py
@@ -15,6 +15,7 @@
 HB = 8
 LATER = 6
 EARLY = 3
+PARTS = 4
 TOK = 128
 N_CTX = 32
 SCALE = (DN + DR) ** -0.5
@@ -60,43 +61,45 @@
     mul, offs, corr, w, q, cot, scaled, rope, bias, acc, racc = refs
     zero = jnp.zeros((TOK, TOK), BF16)
     proj = dot_n(scaled[part, :], w[...]).astype(BF16)
-    dkvs = []
-    rtotal = None
+    dkvs, all_ds, rots = [], [], []
     for pair in range(HB // 2):
         base = 2 * pair * (DN + DR)
         rot = jnp.concatenate(
             [q[:, base + DN : base + DN + DR], q[:, base + 2 * DN + DR : base + 2 * (DN + DR)]], 0
         )
+        rots.append(rot)
         srot = dot_t(rope[part, :], rot)
-        dss = []
-        for j in range(2):
-            i = 2 * pair + j
+        both = (2 * pair, 2 * pair + 1)
+        diags, phs, sds, dss, pbs = [], [], [], [], []
+        for i in both:
             qn = q[:, i * (DN + DR) : i * (DN + DR) + DN]
             ct = cot[:, i * DV : (i + 1) * DV]
-            diag = jnp.concatenate(
-                [jnp.concatenate([qn, zero], 1), jnp.concatenate([zero, ct], 1)], 0
+            diags.append(
+                jnp.concatenate(
+                    [jnp.concatenate([qn, zero], 1), jnp.concatenate([zero, ct], 1)], 0
+                )
             )
+            phs.append(proj[:, i * (DN + DV) : (i + 1) * (DN + DV)])
+            sds.append(dot_t(phs[-1], diags[-1]))
+        for j, i in enumerate(both):
             head = step * HB + i
             off = offs[pl.ds(head, 1), :] * LOG2E
             cor = corr[pl.ds(head, 1), :]
-            ph = proj[:, i * (DN + DV) : (i + 1) * (DN + DV)]
-            sd = dot_t(ph, diag)
-            s = sd[:, :TOK] + srot[:, j * TOK : (j + 1) * TOK]
+            s = sds[j][:, :TOK] + srot[:, j * TOK : (j + 1) * TOK]
             p = jnp.exp2(s * (SCALE * LOG2E) + (bias[part, :] - off))
-            ds = (p * (sd[:, TOK:] - cor)).astype(BF16)
-            pb = p.astype(BF16)
-            dkv = dot_n(jnp.concatenate([ds, pb], 1), diag)
+            dss.append((p * (sds[j][:, TOK:] - cor)).astype(BF16))
+            pbs.append(p.astype(BF16))
+        for j, i in enumerate(both):
+            dkv = dot_n(jnp.concatenate([dss[j], pbs[j]], 1), diags[j])
             dkvs.append((dkv * mul[...]).astype(BF16))
-            dss.append(ds)
             if keep is None:
-                kr = jnp.concatenate([ph[:, :DN], rope[part, :]], 1)
-                dq[:, i * (DN + DR) : (i + 1) * (DN + DR)] = (dot_l(ds, kr) * SCALE).astype(BF16)
+                kr = jnp.concatenate([phs[j][:, :DN], rope[part, :]], 1)
+                dq[:, i * (DN + DR) : (i + 1) * (DN + DR)] = (dot_l(dss[j], kr) * SCALE).astype(BF16)
             else:
-                keep(2 * i, ds)
-                keep(2 * i + 1, ph[:, :DN])
-        rpart = dot_n(jnp.concatenate(dss, 1), rot)
-        rtotal = rpart if rtotal is None else rtotal + rpart
-    racc[part, :] += rtotal
+                keep(i, dss[j])
+                keep(HB + i, phs[j][:, :DN])
+        all_ds += dss
+    racc[part, :] += dot_n(jnp.concatenate(all_ds, 1), jnp.concatenate(rots, 0))
     acc[part, :] += dot_t(jnp.concatenate(dkvs, 1), w[...])
 
 
@@ -188,14 +191,22 @@
         gain_rows[...] = jnp.broadcast_to(total[None], gain_rows.shape)
 
 
-def later_kernel(stored, rope, _, dq):
+def later_kernel(*refs):
+    rope, _, dq = refs[PARTS:]
+    each = 2 * HB // PARTS
     for i in range(HB):
-        kr = jnp.concatenate([stored[0, 2 * i + 1], rope[...]], 1)
-        dq[:, i * (DN + DR) : (i + 1) * (DN + DR)] = (dot_l(stored[0, 2 * i], kr) * SCALE).astype(BF16)
+        ds = refs[i // each][0, i % each]
+        keys = refs[(HB + i) // each][0, i % each]
+        kr = jnp.concatenate([keys, rope[...]], 1)
+        dq[:, i * (DN + DR) : (i + 1) * (DN + DR)] = (dot_l(ds, kr) * SCALE).astype(BF16)
 
 
 def in_vmem(x):
     return pltpu.with_memory_space_constraint(x, pltpu.VMEM)
+
+
+def stored_part(part, i):
+    return i, part, 0, 0
 
 
 def later_queries(stored, rope, dq):
@@ -205,19 +216,22 @@
         grid=(LATER,),
         out_shape=jax.ShapeDtypeStruct(dq.shape, dq.dtype),
         in_specs=[
-            pl.BlockSpec((1, 2 * HB, rows, TOK), lambda i: (i, 0, 0, 0)),
+            *[
+                pl.BlockSpec((1, 2 * HB // PARTS, rows, TOK), functools.partial(stored_part, j))
+                for j in range(PARTS)
+            ],
             pl.BlockSpec((rows, DR), lambda i: (0, 0)),
             pl.BlockSpec(memory_space=pl.ANY),
         ],
         out_specs=pl.BlockSpec((TOK, HB * (DN + DR)), lambda i: (0, i)),
-        input_output_aliases={2: 0},
+        input_output_aliases={PARTS + 1: 0},
         compiler_params=pltpu.CompilerParams(vmem_limit_bytes=56 * 2**20),
         cost_estimate=pl.CostEstimate(
             flops=2 * LATER * HB * TOK * rows * (DN + DR),
             bytes_accessed=LATER * HB * TOK * (4 * rows + 2 * (DN + DR)),
             transcendentals=0,
         ),
-    )(stored, in_vmem(rope), dq)
+    )(*[stored] * PARTS, in_vmem(rope), dq)
 
 
 def whole(*shape):

time: 96 us -> 92.3 us (0.961)
  Pallas kernels: 65.2 us -> 61.4 us
  waiting for transfers between devices: 3.74 us -> 5.42 us
  starting transfers between devices: 24.5 us -> 22.9 us
    pallas_call x1, Pallas kernels: 44.7 us -> 42.6 us  [visits(): pl.pallas_call(functools.partial(kernel, steps), grid=(H // HB,), out_sha...]
    ppermute x8, starting transfers between devices: 16 us -> 14.4 us  [moved(): return lax.ppermute(x, 'ctx', [((i - distance) % n, i) for i in range(n)])]
    pallas_call x1, Pallas kernels: 10.9 us -> 9.32 us  [early_visit(): pl.pallas_call(early_kernel, grid=(EARLY,), out_shape=[jax.ShapeDtypeStru...]
    ppermute x8, waiting for transfers between devices: 2.87 us -> 4.41 us  [moved(): return lax.ppermute(x, 'ctx', [((i - distance) % n, i) for i in range(n)])]
  transfers between devices with their start and end apart: 9 -> 9, of which waited for: 2 -> 2; matrix products, arithmetic and copies ran while one was open for 1% -> 1% of each run, Pallas kernels for 21% -> 20%
where the time goes in v4:
time: 92.3 us; the launch traced here: 92.1 us
  Pallas kernels  61.4 us (67%)
  starting transfers between devices  22.9 us (25%)
  waiting for transfers between devices  5.42 us (6%)
  other arithmetic  1.65 us (2%)
    pallas_call x1, Pallas kernels, visits(): pl.pallas_call(functools.partial(kernel, steps), grid=(H // HB,), out_sha...  42.6 us
    ppermute x8, starting transfers between devices, moved(): return lax.ppermute(x, 'ctx', [((i - distance) % n, i) for i in range(n)])  14.4 us
    pallas_call x1, Pallas kernels, later_queries(): pl.pallas_call(later_kernel, grid=(LATER,), out_shape=jax.ShapeDtypeStruc...  9.49 us
    pallas_call x1, Pallas kernels, early_visit(): pl.pallas_call(early_kernel, grid=(EARLY,), out_shape=[jax.ShapeDtypeStru...  9.32 us
    all_to_all x1, starting transfers between devices, everywhere_sum(): moved_rows = lax.all_to_all(rows, ('ctx', 'dp'), 0, 0, tiled=True)  8.46 us
    ppermute x8, waiting for transfers between devices, moved(): return lax.ppermute(x, 'ctx', [((i - distance) % n, i) for i in range(n)])  4.41 us
  transfers between devices with their start and end apart: 9, of which 2 were waited for; matrix products, arithmetic and copies ran while one was open for 1% of the time, Pallas kernels for 20%

profile of v4, /device:TPU:1, one launch (start us, length us, event | category | flops | bytes accessed | tf_op | source)
XLA Modules:
  0.0 92.1 jit_solution(7539031356767866211)
XLA Ops:
  0.6 2.1 %collective-permute-start = (bf16[576,128]{1,0:T(8,128)(2,1)}, bf16[576,128]{1,0:T(8,128)(2,1)S(1)}, u32[]{:S(2)}, u32[]{:S(2)}) collective-permute-start(bf16[576,128]{1,0:T(8,128)(2,1)} %bitcast.19), channel_id=1, source_target_pairs={{124,0},{0,4},{4,8},{8,12},{12,16},{16,20},{20,24},{24,28},{28,32}... | collective-permute-start | bytes 442376 | tf_op jit(solution)/shard_map/ppermute | solution.py:341
  2.7 2.5 %collective-permute-start.1 = (bf16[576,128]{1,0:T(8,128)(2,1)}, bf16[576,128]{1,0:T(8,128)(2,1)S(1)}, u32[]{:S(2)}, u32[]{:S(2)}) collective-permute-start(bf16[576,128]{1,0:T(8,128)(2,1)} %bitcast.20), channel_id=1, source_target_pairs={{120,0},{124,4},{0,8},{4,12},{8,16},{12,20},{16,24},{20,28},{24,32... | collective-permute-start | bytes 442376 | tf_op jit(solution)/shard_map/ppermute | solution.py:341
  5.2 4.5 %collective-permute-start.2 = (bf16[576,128]{1,0:T(8,128)(2,1)}, bf16[576,128]{1,0:T(8,128)(2,1)S(1)}, u32[]{:S(2)}, u32[]{:S(2)}) collective-permute-start(bf16[576,128]{1,0:T(8,128)(2,1)} %bitcast.21), channel_id=1, source_target_pairs={{116,0},{120,4},{124,8},{0,12},{4,16},{8,20},{12,24},{16,28},{20,3... | collective-permute-start | bytes 442376 | tf_op jit(solution)/shard_map/ppermute | solution.py:341
  9.7 0.4 collective-permute-start.3
  10.0 9.3 %shard_map.103 = (bf16[6,16,640,128]{3,2,1,0:T(8,128)(2,1)}, f32[128,512]{1,0:T(8,128)S(1)}, f32[128,64]{1,0:T(8,128)S(1)}) custom-call(s32[1,64]{1,0:T(1,128)} %order.3, s32[1]{0:T(128)} %bitcast.member, f32[1,512]{1,0:T(1,128)} %bitcast.29, f32[1,256]{1,0:T(1,128)} %constant.4.clone.1.mul, f32[64,128]{1,0:T(8,128)} %bitcast.25, f32[64,128]{1,0:T(8,128)} %bitcast.27, ...), custom_call_target="tpu_custom_call" | custom-call | flops 2113929216 | bytes 8650752 | tf_op jit(solution)/shard_map/pallas_call | solution.py:264
  19.4 0.0 collective-permute-done.refs_1_
  19.4 0.0 collective-permute-done.1.refs_2_
  19.4 0.0 collective-permute-done.2.refs_3_
  19.4 4.4 %collective-permute-done.3.refs_4_ = bf16[576,128]{1,0:T(8,128)(2,1)S(1)} collective-permute-done((bf16[576,128]{1,0:T(8,128)(2,1)}, bf16[576,128]{1,0:T(8,128)(2,1)S(1)}, u32[]{:S(2)}, u32[]{:S(2)}) %collective-permute-start.3) | collective-permute-done | bytes 147488 | tf_op jit(solution)/shard_map/ppermute | solution.py:341
  23.8 0.0 copy-start.1
  23.8 42.6 %shard_map.104 = (bf16[128,12288]{1,0:T(8,128)(2,1)}, bf16[6,16,640,128]{3,2,1,0:T(8,128)(2,1)}, bf16[640,64]{1,0:T(8,128)(2,1)S(1)}, f32[576,128]{1,0:T(8,128)}...) custom-call(s32[1,64]{1,0:T(1,128)} %order.3, ...), custom_call_target="tpu_custom_call", output_to_operand_aliasing={{1}: (16, {})} | custom-call | flops 28185722880 | bytes 23068672 | tf_op jit(solution)/shard_map/pallas_call | solution.py:293
  66.4 0.1 collective-permute-start.4
  66.5 3.1 %collective-permute-start.5 = (bf16[576,128]{1,0:T(8,128)(2,1)S(1)}, bf16[576,128]{1,0:T(8,128)(2,1)S(1)}, u32[]{:S(2)}, u32[]{:S(2)}) collective-permute-start(bf16[576,128]{1,0:T(8,128)(2,1)S(1)} %get-tuple-element.23), channel_id=1, source_target_pairs={{8,0},{12,4},{16,8},{20,12},{24,16},{28,20},{32,24},{36,28},{40,32... | collective-permute-start | bytes 442376 | tf_op jit(solution)/shard_map/ppermute | solution.py:341
  69.6 0.9 collective-permute-start.6
  70.5 0.9 collective-permute-start.7
  71.4 0.0 copy-done.1
  71.4 8.5 %all-to-all-start = ((f32[128,1,512]{2,1,0:T(1,128)}), f32[128,1,512]{2,1,0:T(1,128)S(1)}, u32[]{:S(2)}, u32[]{:S(2)}) async-start(f32[128,1,512]{2,1,0:T(1,128)} %get-tuple-element.26), calls=%async_computation | async-start | bytes 524288 | tf_op jit(solution)/shard_map/all_to_all | solution.py:335
  79.9 0.0 copy-start
  79.9 9.5 %shard_map.105 = bf16[128,12288]{1,0:T(8,128)(2,1)} custom-call(bf16[6,16,640,128]{3,2,1,0:T(8,128)(2,1)} %get-tuple-element.18.refs_0_.refs_1_.refs_2_.refs_3_, bf16[6,16,640,128]{3,2,1,0:T(8,128)(2,1)} %get-tuple-element.18.refs_0_.refs_1_.refs_2_.refs_3_, ...), custom_call_target="tpu_custom_call", output_to_operand_aliasing={{}: (5, {})} | custom-call | flops 1509949440 | bytes 18087936 | tf_op jit(solution)/shard_map/pallas_call | solution.py:214
  89.4 0.0 collective-permute-done.4
  89.4 0.0 collective-permute-done.5
  89.4 0.0 collective-permute-done.6
  89.4 0.0 collective-permute-done.7
  89.4 0.0 copy-done
  89.4 0.9 multiply_bitcast_fusion
  90.3 1.0 %all-to-all-done = f32[128,1,512]{2,1,0:T(1,128)S(1)} async-done(((f32[128,1,512]{2,1,0:T(1,128)}), f32[128,1,512]{2,1,0:T(1,128)S(1)}, u32[]{:S(2)}, u32[]{:S(2)}) %all-to-all-start) | async-done | bytes 262176 | tf_op jit(solution)/shard_map/all_to_all | solution.py:335
  91.3 0.8 reduce_sum.9
  (1 shorter events, 0.0 us)
Async XLA Ops:
  0.6 18.7 %collective-permute-start = (bf16[576,128]{1,0:T(8,128)(2,1)}, bf16[576,128]{1,0:T(8,128)(2,1)S(1)}, u32[]{:S(2)}, u32[]{:S(2)}) collective-permute-start(bf16[576,128]{1,0:T(8,128)(2,1)} %bitcast.19), channel_id=1, source_target_pairs={{124,0},{0,4},{4,8},{8,12},{12,16},{16,20},{20,24},{24,28},{28,32}... | collective-permute-start | bytes 442376 | tf_op jit(solution)/shard_map/ppermute | solution.py:341
  2.7 16.6 %collective-permute-start.1 = (bf16[576,128]{1,0:T(8,128)(2,1)}, bf16[576,128]{1,0:T(8,128)(2,1)S(1)}, u32[]{:S(2)}, u32[]{:S(2)}) collective-permute-start(bf16[576,128]{1,0:T(8,128)(2,1)} %bitcast.20), channel_id=1, source_target_pairs={{120,0},{124,4},{0,8},{4,12},{8,16},{12,20},{16,24},{20,28},{24,32... | collective-permute-start | bytes 442376 | tf_op jit(solution)/shard_map/ppermute | solution.py:341
  5.2 14.2 %collective-permute-start.2 = (bf16[576,128]{1,0:T(8,128)(2,1)}, bf16[576,128]{1,0:T(8,128)(2,1)S(1)}, u32[]{:S(2)}, u32[]{:S(2)}) collective-permute-start(bf16[576,128]{1,0:T(8,128)(2,1)} %bitcast.21), channel_id=1, source_target_pairs={{116,0},{120,4},{124,8},{0,12},{4,16},{8,20},{12,24},{16,28},{20,3... | collective-permute-start | bytes 442376 | tf_op jit(solution)/shard_map/ppermute | solution.py:341
  9.7 14.1 %collective-permute-start.3 = (bf16[576,128]{1,0:T(8,128)(2,1)}, bf16[576,128]{1,0:T(8,128)(2,1)S(1)}, u32[]{:S(2)}, u32[]{:S(2)}) collective-permute-start(bf16[576,128]{1,0:T(8,128)(2,1)} %bitcast.22), channel_id=1, source_target_pairs={{112,0},{116,4},{120,8},{124,12},{0,16},{4,20},{8,24},{12,28},{16,... | collective-permute-start | bytes 442376 | tf_op jit(solution)/shard_map/ppermute | solution.py:341
  23.8 47.6 %copy-start.1 = (f32[512]{0:T(512)S(1)}, f32[512]{0:T(512)}, u32[]{:S(2)}) copy-start(f32[512]{0:T(512)} %param.14) | copy-start | bytes 6148
  66.4 23.0 %collective-permute-start.4 = (bf16[576,128]{1,0:T(8,128)(2,1)S(1)}, bf16[576,128]{1,0:T(8,128)(2,1)S(1)}, u32[]{:S(2)}, u32[]{:S(2)}) collective-permute-start(bf16[576,128]{1,0:T(8,128)(2,1)S(1)} %get-tuple-element.22), channel_id=1, source_target_pairs={{4,0},{8,4},{12,8},{16,12},{20,16},{24,20},{28,24},{32,28},{36,32}... | collective-permute-start | bytes 442376 | tf_op jit(solution)/shard_map/ppermute | solution.py:341
  66.5 22.9 %collective-permute-start.5 = (bf16[576,128]{1,0:T(8,128)(2,1)S(1)}, bf16[576,128]{1,0:T(8,128)(2,1)S(1)}, u32[]{:S(2)}, u32[]{:S(2)}) collective-permute-start(bf16[576,128]{1,0:T(8,128)(2,1)S(1)} %get-tuple-element.23), channel_id=1, source_target_pairs={{8,0},{12,4},{16,8},{20,12},{24,16},{28,20},{32,24},{36,28},{40,32... | collective-permute-start | bytes 442376 | tf_op jit(solution)/shard_map/ppermute | solution.py:341
  69.6 19.8 %collective-permute-start.6 = (bf16[576,128]{1,0:T(8,128)(2,1)S(1)}, bf16[576,128]{1,0:T(8,128)(2,1)S(1)}, u32[]{:S(2)}, u32[]{:S(2)}) collective-permute-start(bf16[576,128]{1,0:T(8,128)(2,1)S(1)} %get-tuple-element.24), channel_id=1, source_target_pairs={{12,0},{16,4},{20,8},{24,12},{28,16},{32,20},{36,24},{40,28},{44,3... | collective-permute-start | bytes 442376 | tf_op jit(solution)/shard_map/ppermute | solution.py:341
  70.5 18.9 %collective-permute-start.7 = (bf16[576,128]{1,0:T(8,128)(2,1)S(1)}, bf16[576,128]{1,0:T(8,128)(2,1)S(1)}, u32[]{:S(2)}, u32[]{:S(2)}) collective-permute-start(bf16[576,128]{1,0:T(8,128)(2,1)S(1)} %get-tuple-element.25), channel_id=1, source_target_pairs={{16,0},{20,4},{24,8},{28,12},{32,16},{36,20},{40,24},{44,28},{48,3... | collective-permute-start | bytes 442376 | tf_op jit(solution)/shard_map/ppermute | solution.py:341
  71.4 19.9 %all-to-all-start = ((f32[128,1,512]{2,1,0:T(1,128)}), f32[128,1,512]{2,1,0:T(1,128)S(1)}, u32[]{:S(2)}, u32[]{:S(2)}) async-start(f32[128,1,512]{2,1,0:T(1,128)} %get-tuple-element.26), calls=%async_computation | async-start | bytes 524288 | tf_op jit(solution)/shard_map/all_to_all | solution.py:335
  79.9 9.5 %copy-start = (f32[576,128]{1,0:T(8,128)S(1)}, f32[576,128]{1,0:T(8,128)}, u32[]{:S(2)}) copy-start(f32[576,128]{1,0:T(8,128)} %get-tuple-element.21) | copy-start | bytes 884740

commit v5 on v4

--- a/solution.py
+++ b/solution.py
@@ -298,9 +298,9 @@
             jax.ShapeDtypeStruct(stored.shape, BF16),
             pltpu.VMEM((rows, DR), BF16),
         ]
-        + [jax.ShapeDtypeStruct((KVL + DR, TOK), F32)]
+        + [pltpu.VMEM((KVL + DR, TOK), F32)]
         + [pltpu.VMEM((KVL + DR, TOK), BF16)] * (n - 1)
-        + [jax.ShapeDtypeStruct((peers, 1, KVL), F32)],
+        + [pltpu.VMEM((peers, 1, KVL), F32)],
         in_specs=inputs_specs(n) + [whole(TOK, KVL), whole(TOK, DR), anywhere],
         out_specs=[
             pl.BlockSpec((TOK, HB * (DN + DR)), lambda i: (0, jnp.maximum(i, LATER))),

time: 92.3 us -> 92.2 us (level)
  no operation moved by 1% of the time
where the time goes in v5:
time: 92.2 us; the launch traced here: 92 us
  Pallas kernels  61.3 us (66%)
  starting transfers between devices  23 us (25%)
  waiting for transfers between devices  5.43 us (6%)
  other arithmetic  1.65 us (2%)
    pallas_call x1, Pallas kernels, visits(): pl.pallas_call(functools.partial(kernel, steps), grid=(H // HB,), out_sha...  42.4 us
    ppermute x8, starting transfers between devices, moved(): return lax.ppermute(x, 'ctx', [((i - distance) % n, i) for i in range(n)])  14.5 us
    pallas_call x1, Pallas kernels, later_queries(): pl.pallas_call(later_kernel, grid=(LATER,), out_shape=jax.ShapeDtypeStruc...  9.45 us
    pallas_call x1, Pallas kernels, early_visit(): pl.pallas_call(early_kernel, grid=(EARLY,), out_shape=[jax.ShapeDtypeStru...  9.36 us
    all_to_all x1, starting transfers between devices, everywhere_sum(): moved_rows = lax.all_to_all(rows, ('ctx', 'dp'), 0, 0, tiled=True)  8.46 us
    ppermute x8, waiting for transfers between devices, moved(): return lax.ppermute(x, 'ctx', [((i - distance) % n, i) for i in range(n)])  4.36 us
  transfers between devices with their start and end apart: 9, of which 2 were waited for; matrix products, arithmetic and copies ran while one was open for 1% of the time, Pallas kernels for 20%

profile of v5, /device:TPU:1, one launch (start us, length us, event | category | flops | bytes accessed | tf_op | source)
XLA Modules:
  0.0 92.0 jit_solution(13473222028636307334)
XLA Ops:
  0.6 2.1 %collective-permute-start = (bf16[576,128]{1,0:T(8,128)(2,1)}, bf16[576,128]{1,0:T(8,128)(2,1)S(1)}, u32[]{:S(2)}, u32[]{:S(2)}) collective-permute-start(bf16[576,128]{1,0:T(8,128)(2,1)} %bitcast.19), channel_id=1, source_target_pairs={{124,0},{0,4},{4,8},{8,12},{12,16},{16,20},{20,24},{24,28},{28,32}... | collective-permute-start | bytes 442376 | tf_op jit(solution)/shard_map/ppermute | solution.py:341
  2.7 2.5 %collective-permute-start.1 = (bf16[576,128]{1,0:T(8,128)(2,1)}, bf16[576,128]{1,0:T(8,128)(2,1)S(1)}, u32[]{:S(2)}, u32[]{:S(2)}) collective-permute-start(bf16[576,128]{1,0:T(8,128)(2,1)} %bitcast.20), channel_id=1, source_target_pairs={{120,0},{124,4},{0,8},{4,12},{8,16},{12,20},{16,24},{20,28},{24,32... | collective-permute-start | bytes 442376 | tf_op jit(solution)/shard_map/ppermute | solution.py:341
  5.2 4.5 %collective-permute-start.2 = (bf16[576,128]{1,0:T(8,128)(2,1)}, bf16[576,128]{1,0:T(8,128)(2,1)S(1)}, u32[]{:S(2)}, u32[]{:S(2)}) collective-permute-start(bf16[576,128]{1,0:T(8,128)(2,1)} %bitcast.21), channel_id=1, source_target_pairs={{116,0},{120,4},{124,8},{0,12},{4,16},{8,20},{12,24},{16,28},{20,3... | collective-permute-start | bytes 442376 | tf_op jit(solution)/shard_map/ppermute | solution.py:341
  9.7 0.4 collective-permute-start.3
  10.0 9.4 %shard_map.103 = (bf16[6,16,640,128]{3,2,1,0:T(8,128)(2,1)}, f32[128,512]{1,0:T(8,128)S(1)}, f32[128,64]{1,0:T(8,128)S(1)}) custom-call(s32[1,64]{1,0:T(1,128)} %order.3, s32[1]{0:T(128)} %bitcast.member, f32[1,512]{1,0:T(1,128)} %bitcast.29, f32[1,256]{1,0:T(1,128)} %constant.4.clone.1.mul, f32[64,128]{1,0:T(8,128)} %bitcast.25, f32[64,128]{1,0:T(8,128)} %bitcast.27, ...), custom_call_target="tpu_custom_call" | custom-call | flops 2113929216 | bytes 8650752 | tf_op jit(solution)/shard_map/pallas_call | solution.py:264
  19.4 0.0 collective-permute-done.refs_1_
  19.4 0.0 collective-permute-done.1.refs_2_
  19.4 0.0 collective-permute-done.2.refs_3_
  19.4 4.3 %collective-permute-done.3.refs_4_ = bf16[576,128]{1,0:T(8,128)(2,1)S(1)} collective-permute-done((bf16[576,128]{1,0:T(8,128)(2,1)}, bf16[576,128]{1,0:T(8,128)(2,1)S(1)}, u32[]{:S(2)}, u32[]{:S(2)}) %collective-permute-start.3) | collective-permute-done | bytes 147488 | tf_op jit(solution)/shard_map/ppermute | solution.py:341
  23.8 0.0 copy-start
  23.8 42.4 %shard_map.104 = (bf16[128,12288]{1,0:T(8,128)(2,1)}, bf16[6,16,640,128]{3,2,1,0:T(8,128)(2,1)}, bf16[640,64]{1,0:T(8,128)(2,1)S(1)}, f32[576,128]{1,0:T(8,128)S...) custom-call(s32[1,64]{1,0:T(1,128)} %order.3, ...), custom_call_target="tpu_custom_call", output_to_operand_aliasing={{1}: (16, {})} | custom-call | flops 28185722880 | bytes 23068672 | tf_op jit(solution)/shard_map/pallas_call | solution.py:293
  66.2 0.2 collective-permute-start.4
  66.4 3.0 %collective-permute-start.5 = (bf16[576,128]{1,0:T(8,128)(2,1)S(1)}, bf16[576,128]{1,0:T(8,128)(2,1)S(1)}, u32[]{:S(2)}, u32[]{:S(2)}) collective-permute-start(bf16[576,128]{1,0:T(8,128)(2,1)S(1)} %get-tuple-element.23), channel_id=1, source_target_pairs={{8,0},{12,4},{16,8},{20,12},{24,16},{28,20},{32,24},{36,28},{40,32... | collective-permute-start | bytes 442376 | tf_op jit(solution)/shard_map/ppermute | solution.py:341
  69.5 0.9 collective-permute-start.6
  70.4 1.0 %collective-permute-start.7 = (bf16[576,128]{1,0:T(8,128)(2,1)S(1)}, bf16[576,128]{1,0:T(8,128)(2,1)S(1)}, u32[]{:S(2)}, u32[]{:S(2)}) collective-permute-start(bf16[576,128]{1,0:T(8,128)(2,1)S(1)} %get-tuple-element.25), channel_id=1, source_target_pairs={{16,0},{20,4},{24,8},{28,12},{32,16},{36,20},{40,24},{44,28},{48,3... | collective-permute-start | bytes 442376 | tf_op jit(solution)/shard_map/ppermute | solution.py:341
  71.3 0.0 copy-done
  71.3 8.5 %all-to-all-start = ((f32[128,1,512]{2,1,0:T(1,128)}), f32[128,1,512]{2,1,0:T(1,128)S(1)}, u32[]{:S(2)}, u32[]{:S(2)}) async-start(f32[128,1,512]{2,1,0:T(1,128)} %get-tuple-element.26), calls=%async_computation | async-start | bytes 524288 | tf_op jit(solution)/shard_map/all_to_all | solution.py:335
  79.8 9.5 %shard_map.105 = bf16[128,12288]{1,0:T(8,128)(2,1)} custom-call(bf16[6,16,640,128]{3,2,1,0:T(8,128)(2,1)} %get-tuple-element.18.refs_0_.refs_1_.refs_2_.refs_3_, bf16[6,16,640,128]{3,2,1,0:T(8,128)(2,1)} %get-tuple-element.18.refs_0_.refs_1_.refs_2_.refs_3_, ...), custom_call_target="tpu_custom_call", output_to_operand_aliasing={{}: (5, {})} | custom-call | flops 1509949440 | bytes 18087936 | tf_op jit(solution)/shard_map/pallas_call | solution.py:214
  89.3 0.0 collective-permute-done.4
  89.3 0.0 collective-permute-done.5
  89.3 0.0 collective-permute-done.6
  89.3 0.0 collective-permute-done.7
  89.3 0.9 multiply_bitcast_fusion
  90.2 1.1 %all-to-all-done = f32[128,1,512]{2,1,0:T(1,128)S(1)} async-done(((f32[128,1,512]{2,1,0:T(1,128)}), f32[128,1,512]{2,1,0:T(1,128)S(1)}, u32[]{:S(2)}, u32[]{:S(2)}) %all-to-all-start) | async-done | bytes 262176 | tf_op jit(solution)/shard_map/all_to_all | solution.py:335
  91.2 0.8 reduce_sum.9
  (1 shorter events, 0.0 us)
Async XLA Ops:
  0.6 18.8 %collective-permute-start = (bf16[576,128]{1,0:T(8,128)(2,1)}, bf16[576,128]{1,0:T(8,128)(2,1)S(1)}, u32[]{:S(2)}, u32[]{:S(2)}) collective-permute-start(bf16[576,128]{1,0:T(8,128)(2,1)} %bitcast.19), channel_id=1, source_target_pairs={{124,0},{0,4},{4,8},{8,12},{12,16},{16,20},{20,24},{24,28},{28,32}... | collective-permute-start | bytes 442376 | tf_op jit(solution)/shard_map/ppermute | solution.py:341
  2.7 16.7 %collective-permute-start.1 = (bf16[576,128]{1,0:T(8,128)(2,1)}, bf16[576,128]{1,0:T(8,128)(2,1)S(1)}, u32[]{:S(2)}, u32[]{:S(2)}) collective-permute-start(bf16[576,128]{1,0:T(8,128)(2,1)} %bitcast.20), channel_id=1, source_target_pairs={{120,0},{124,4},{0,8},{4,12},{8,16},{12,20},{16,24},{20,28},{24,32... | collective-permute-start | bytes 442376 | tf_op jit(solution)/shard_map/ppermute | solution.py:341
  5.2 14.2 %collective-permute-start.2 = (bf16[576,128]{1,0:T(8,128)(2,1)}, bf16[576,128]{1,0:T(8,128)(2,1)S(1)}, u32[]{:S(2)}, u32[]{:S(2)}) collective-permute-start(bf16[576,128]{1,0:T(8,128)(2,1)} %bitcast.21), channel_id=1, source_target_pairs={{116,0},{120,4},{124,8},{0,12},{4,16},{8,20},{12,24},{16,28},{20,3... | collective-permute-start | bytes 442376 | tf_op jit(solution)/shard_map/ppermute | solution.py:341
  9.7 14.1 %collective-permute-start.3 = (bf16[576,128]{1,0:T(8,128)(2,1)}, bf16[576,128]{1,0:T(8,128)(2,1)S(1)}, u32[]{:S(2)}, u32[]{:S(2)}) collective-permute-start(bf16[576,128]{1,0:T(8,128)(2,1)} %bitcast.22), channel_id=1, source_target_pairs={{112,0},{116,4},{120,8},{124,12},{0,16},{4,20},{8,24},{12,28},{16,... | collective-permute-start | bytes 442376 | tf_op jit(solution)/shard_map/ppermute | solution.py:341
  23.8 47.6 %copy-start = (f32[512]{0:T(512)S(1)}, f32[512]{0:T(512)}, u32[]{:S(2)}) copy-start(f32[512]{0:T(512)} %param.14) | copy-start | bytes 6148
  66.2 23.0 %collective-permute-start.4 = (bf16[576,128]{1,0:T(8,128)(2,1)S(1)}, bf16[576,128]{1,0:T(8,128)(2,1)S(1)}, u32[]{:S(2)}, u32[]{:S(2)}) collective-permute-start(bf16[576,128]{1,0:T(8,128)(2,1)S(1)} %get-tuple-element.22), channel_id=1, source_target_pairs={{4,0},{8,4},{12,8},{16,12},{20,16},{24,20},{28,24},{32,28},{36,32}... | collective-permute-start | bytes 442376 | tf_op jit(solution)/shard_map/ppermute | solution.py:341
  66.4 22.8 %collective-permute-start.5 = (bf16[576,128]{1,0:T(8,128)(2,1)S(1)}, bf16[576,128]{1,0:T(8,128)(2,1)S(1)}, u32[]{:S(2)}, u32[]{:S(2)}) collective-permute-start(bf16[576,128]{1,0:T(8,128)(2,1)S(1)} %get-tuple-element.23), channel_id=1, source_target_pairs={{8,0},{12,4},{16,8},{20,12},{24,16},{28,20},{32,24},{36,28},{40,32... | collective-permute-start | bytes 442376 | tf_op jit(solution)/shard_map/ppermute | solution.py:341
  69.5 19.8 %collective-permute-start.6 = (bf16[576,128]{1,0:T(8,128)(2,1)S(1)}, bf16[576,128]{1,0:T(8,128)(2,1)S(1)}, u32[]{:S(2)}, u32[]{:S(2)}) collective-permute-start(bf16[576,128]{1,0:T(8,128)(2,1)S(1)} %get-tuple-element.24), channel_id=1, source_target_pairs={{12,0},{16,4},{20,8},{24,12},{28,16},{32,20},{36,24},{40,28},{44,3... | collective-permute-start | bytes 442376 | tf_op jit(solution)/shard_map/ppermute | solution.py:341
  70.4 18.9 %collective-permute-start.7 = (bf16[576,128]{1,0:T(8,128)(2,1)S(1)}, bf16[576,128]{1,0:T(8,128)(2,1)S(1)}, u32[]{:S(2)}, u32[]{:S(2)}) collective-permute-start(bf16[576,128]{1,0:T(8,128)(2,1)S(1)} %get-tuple-element.25), channel_id=1, source_target_pairs={{16,0},{20,4},{24,8},{28,12},{32,16},{36,20},{40,24},{44,28},{48,3... | collective-permute-start | bytes 442376 | tf_op jit(solution)/shard_map/ppermute | solution.py:341
  71.3 19.9 %all-to-all-start = ((f32[128,1,512]{2,1,0:T(1,128)}), f32[128,1,512]{2,1,0:T(1,128)S(1)}, u32[]{:S(2)}, u32[]{:S(2)}) async-start(f32[128,1,512]{2,1,0:T(1,128)} %get-tuple-element.26), calls=%async_computation | async-start | bytes 524288 | tf_op jit(solution)/shard_map/all_to_all | solution.py:335
